TPU v7x, 32 devices: a whole 2x2x4 slice. The times are simulated.
32 devices in a mesh: item: 8 (over y, x, core), tbl: 4 (over z).
Axes of the slice: x: 2, y: 2, z: 4, core: 2. Of those that a mesh axis runs over, the one named last changes fastest.
Arguments:
- tables: bfloat16 [8, 8192, 128], P('tbl'), may hold values from -2.5 to 2.5
- feat_ids: int32 [32768, 8, 8], P('item', 'tbl'), may hold values from 0 to 8191
- bag_lens: int32 [32768, 8], P('item', 'tbl'), may hold values from 1 to 8
- w_hidden: bfloat16 [1024, 1024], replicated, may hold values from -0.1875 to 0.1875
- b_hidden: float32 [1024], replicated, may hold values from -3 to 3
- w_out: bfloat16 [1024, 256], replicated, may hold values from -0.1875 to 0.1875
- b_out: float32 [256], replicated, may hold values from -3 to 3
- item_vecs: bfloat16 [2048, 256], P('item'), may hold values from -30 to 30
- elig_mask: int32 [64, 16], P(('item', 'tbl')), may hold values from 0 to 1, as said below
- positives: int32 [32768], P(('item', 'tbl')), may hold values from 0 to 2047, as said below
Outputs:
- user_loss: float32 [32768], P(('item', 'tbl'))
- user_grad: float32 [32768, 256], P(('item', 'tbl'))
- item_grad: float32 [2048, 256], P(('item', 'tbl'))
Inputs may be any that keep to these rules, and one draw needn't show every extreme that they name: Every row of elig_mask holds at least one 1. elig_mask[u // 512, positives[u] // 128] = 1 for every user u.
All inputs are finite; a program needn't handle non-finite values.
Results may differ from a plain program's by a relative error of at most 0.03.
Values may be sent and summed in bfloat16 or wider, within the bound.
A program may use at most 64 MiB of HBM per device.

v0:
```python
import math

import jax
import jax.numpy as jnp
from jax import lax
from jax.sharding import PartitionSpec as P

IBLK = 128


masked_value = -1e30


def shifted(value, axis, steps):
    count = lax.axis_size(axis)
    pairs = [(source, (source + steps) % count) for source in range(count)]
    return lax.ppermute(value, axis, pairs)


def pool_block(table, block_ids, block_lens):
    gathered = jnp.take(table, block_ids, axis=0).astype(jnp.float32)
    in_bag = jnp.arange(block_ids.shape[1], dtype=jnp.int32)[None, :] < block_lens[:, None]
    return jnp.sum(jnp.where(in_bag[:, :, None], gathered, 0.0), axis=1).astype(jnp.bfloat16)


def visit_first(running, visiting, first_item, queries, positives, eligible):
    maxima, totals, picked = running
    piece_rows = visiting.shape[0]
    block_rows = queries.shape[0] // eligible.shape[0]
    columns = lax.dynamic_slice_in_dim(eligible, first_item // IBLK, piece_rows // IBLK, 1)
    item_index = first_item + jnp.arange(piece_rows, dtype=jnp.int32)
    results = []
    for user_block in range(eligible.shape[0]):
        row_lower = user_block * block_rows
        block_queries = queries[row_lower : row_lower + block_rows]
        wanted = positives[row_lower : row_lower + block_rows]
        previous = (
            maxima[row_lower : row_lower + block_rows],
            totals[row_lower : row_lower + block_rows],
            picked[row_lower : row_lower + block_rows],
        )
        allowed = jnp.repeat(columns[user_block] > 0, IBLK)

        def update(block_queries=block_queries, wanted=wanted, previous=previous, allowed=allowed):
            scores = jnp.einsum(
                "ud,id->ui", block_queries, visiting, preferred_element_type=jnp.float32
            )
            block_max = jnp.max(jnp.where(allowed[None, :], scores, masked_value), axis=1)
            new_max = jnp.maximum(previous[0], block_max)
            summed = previous[1] * jnp.exp(previous[0] - new_max) + jnp.sum(
                jnp.where(allowed[None, :], jnp.exp(scores - new_max[:, None]), 0.0), axis=1
            )
            chosen = previous[2] + jnp.sum(
                jnp.where(item_index[None, :] == wanted[:, None], scores, 0.0), axis=1
            )
            return (new_max, summed, chosen)

        outcome = update()
        results.append(outcome)
    return tuple((jnp.concatenate([result[member] for result in results]) for member in range(3)))


def visit_second(visiting, first_item, queries, positives, eligible, log_norm):
    piece_rows = visiting.shape[0]
    embed_width = visiting.shape[1]
    block_rows = queries.shape[0] // eligible.shape[0]
    columns = lax.dynamic_slice_in_dim(eligible, first_item // IBLK, piece_rows // IBLK, 1)
    item_index = first_item + jnp.arange(piece_rows, dtype=jnp.int32)
    user_terms = []
    item_term = jnp.zeros((piece_rows, embed_width), jnp.float32)
    for user_block in range(eligible.shape[0]):
        row_lower = user_block * block_rows
        block_queries = queries[row_lower : row_lower + block_rows]
        wanted = positives[row_lower : row_lower + block_rows]
        norm_rows = log_norm[row_lower : row_lower + block_rows]
        allowed = jnp.repeat(columns[user_block] > 0, IBLK)

        def contribute(
            block_queries=block_queries, wanted=wanted, norm_rows=norm_rows, allowed=allowed
        ):
            scores = jnp.einsum(
                "ud,id->ui", block_queries, visiting, preferred_element_type=jnp.float32
            )
            probabilities = jnp.where(allowed[None, :], jnp.exp(scores - norm_rows[:, None]), 0.0)
            target = item_index[None, :] == wanted[:, None]
            signal = (probabilities - target.astype(jnp.float32)).astype(jnp.bfloat16)
            user_part = jnp.einsum(
                "ui,id->ud", signal, visiting, preferred_element_type=jnp.float32
            )
            item_part = jnp.einsum(
                "ui,ud->id", signal, block_queries, preferred_element_type=jnp.float32
            )
            return (user_part, item_part)

        user_part, item_part = contribute()
        user_terms.append(user_part)
        item_term = item_term + item_part
    return (jnp.concatenate(user_terms, axis=0), item_term)


def local(
    tables, feat_ids, bag_lens, w_hidden, b_hidden, w_out, b_out, item_vecs, elig_mask, positives
):
    table_shards = lax.axis_size("tbl")
    group_users = feat_ids.shape[0]
    users_here = group_users // table_shards
    pool_rows = math.gcd(group_users, 512)
    pool_count = group_users // pool_rows
    pooled_list = []
    for feature in range(feat_ids.shape[1]):
        feature_ids = feat_ids[:, feature, :].reshape(pool_count, pool_rows, feat_ids.shape[2])
        feature_lens = bag_lens[:, feature].reshape(pool_count, pool_rows)
        table = tables[feature]
        pooled_blocks = lax.map(
            lambda pair, table=table: pool_block(table, pair[0], pair[1]),
            (feature_ids, feature_lens),
        )
        pooled_list.append(pooled_blocks.reshape(group_users, tables.shape[2]))
    pooled = jnp.stack(pooled_list, axis=1).reshape(
        table_shards, users_here, feat_ids.shape[1], tables.shape[2]
    )
    arrived = lax.all_to_all(pooled, "tbl", split_axis=0, concat_axis=2, tiled=True)
    count_users = arrived.shape[1]
    features = arrived.reshape(count_users, arrived.shape[2] * arrived.shape[3])
    hidden = jnp.maximum(
        jnp.dot(features, w_hidden, preferred_element_type=jnp.float32) + b_hidden, 0.0
    ).astype(jnp.bfloat16)
    queries = (jnp.dot(hidden, w_out, preferred_element_type=jnp.float32) + b_out).astype(
        jnp.bfloat16
    )[None][0]
    cycle_size = lax.axis_size("item")
    my_index = lax.axis_index("item")
    item_rows = item_vecs.shape[0]
    users_count = queries.shape[0]
    running = (
        jnp.full((users_count,), masked_value, jnp.float32),
        jnp.zeros((users_count,), jnp.float32),
        jnp.zeros((users_count,), jnp.float32),
    )
    pieces = (item_vecs,)
    directions = (1,)
    offsets = (0,)

    def move_first(moving):
        return (shifted(moving[0], "item", 1),)

    def move_second(moving, carried_grads):
        moved = (shifted(moving[0], "item", 1),)
        grads_moved = (shifted(carried_grads[0], "item", 1),)
        return (moved, grads_moved)

    def first_items(distance):
        return tuple(
            (
                (my_index - direction * distance) % cycle_size * item_rows + offset
                for direction, offset in zip(directions, offsets)
            )
        )

    for visiting, first_item in zip(pieces, first_items(0)):
        running = visit_first(running, visiting, first_item, queries, positives, elig_mask)

    def lap_one(distance, carried):
        moving, running = carried
        moving = move_first(moving)
        for visiting, first_item in zip(moving, first_items(distance)):
            running = visit_first(running, visiting, first_item, queries, positives, elig_mask)
        return (moving, running)

    moving, running = lax.fori_loop(1, cycle_size, lap_one, (pieces, running))
    maxima, totals, picked = running
    log_norm = maxima + jnp.log(totals)
    user_loss = log_norm - picked

    def lap_two(distance, carried):
        moving, grads_moving, user_grad = carried
        new_grads = []
        for visiting, grad_piece, first_item in zip(moving, grads_moving, first_items(distance)):
            user_term, item_term = visit_second(
                visiting, first_item, queries, positives, elig_mask, log_norm
            )
            user_grad = user_grad + user_term
            new_grads.append(grad_piece + item_term)
        moving, grads_moving = move_second(moving, tuple(new_grads))
        return (moving, grads_moving, user_grad)

    start_grads = tuple(
        (jnp.zeros((visiting.shape[0], item_vecs.shape[1]), jnp.float32) for visiting in pieces)
    )
    start_user = jnp.zeros((users_count, item_vecs.shape[1]), jnp.float32)
    moving, grads_moving, user_grad = lax.fori_loop(
        0, cycle_size, lap_two, (pieces, start_grads, start_user)
    )
    item_total = grads_moving[0]
    item_grad = lax.psum_scatter(item_total, "tbl", scatter_dimension=0, tiled=True)
    return (user_loss, user_grad, item_grad)


def solution(mesh):
    in_specs = (
        P("tbl", None, None),
        P("item", "tbl", None),
        P("item", "tbl"),
        P(),
        P(),
        P(),
        P(),
        P("item", None),
        P(("item", "tbl"), None),
        P(("item", "tbl")),
    )
    out_specs = (P(("item", "tbl")), P(("item", "tbl"), None), P(("item", "tbl"), None))
    return jax.shard_map(local, mesh=mesh, in_specs=in_specs, out_specs=out_specs, check_vma=False)
```

profile of v0, /device:TPU:0, one launch (start us, length us, event | category | flops | bytes accessed | tf_op | source)
XLA Modules:
  0.0 523.0 jit_solution(17820504186756119150)
XLA Ops:
  16.6 141.9 %while.61 = (s32[]{:T(128)}, bf16[8,512,128]{2,1,0:T(8,128)(2,1)}, s32[8,512]{1,0:T(8,128)S(1)}, s32[8,512,8]{2,1,0:T(8,128)}, bf16[8192,128]{1,0:T(8,128)(2,1)}, /*index=5*/s32[]{:T(128)}) while((s32[]{:T(128)}, bf16[8,512,128]{2,1,0:T(8,128)(2,1)}, s32[8,512]{1,0:T(8,128)S(1)}, s32[8,512,8]{2,1,0:T(8,128)}, bf16[8192,128]{1,0:T(8,128)(2,1)}, ...), condition=%wide.region_2.4_spmd, body=%wide.region_0.3_spmd.sunk | while | flops 2064386 | bytes 3676749 | solution.py:114
  17.9 12.9 %gather_fusion = bf16[4096,128]{1,0:T(8,128)(2,1)S(1)} fusion(bf16[8192,128]{1,0:T(8,128)(2,1)} %get-tuple-element.930, s32[4096]{0:T(1024)S(1)} %broadcast_clamp_fusion.4), kind=kCustom, calls=%fused_computation.clone.clone.1 | custom fusion | bytes 2113536 | tf_op jit(solution)/shard_map/while/body/eval_jaxpr/jit(_take)/gather | solution.py:21
  35.6 12.9 %gather_fusion = bf16[4096,128]{1,0:T(8,128)(2,1)S(1)} fusion(bf16[8192,128]{1,0:T(8,128)(2,1)} %get-tuple-element.930, s32[4096]{0:T(1024)S(1)} %broadcast_clamp_fusion.4), kind=kCustom, calls=%fused_computation.clone.clone.1 | custom fusion | bytes 2113536 | tf_op jit(solution)/shard_map/while/body/eval_jaxpr/jit(_take)/gather | solution.py:21
  53.4 12.9 %gather_fusion = bf16[4096,128]{1,0:T(8,128)(2,1)S(1)} fusion(bf16[8192,128]{1,0:T(8,128)(2,1)} %get-tuple-element.930, s32[4096]{0:T(1024)S(1)} %broadcast_clamp_fusion.4), kind=kCustom, calls=%fused_computation.clone.clone.1 | custom fusion | bytes 2113536 | tf_op jit(solution)/shard_map/while/body/eval_jaxpr/jit(_take)/gather | solution.py:21
  71.1 12.9 %gather_fusion = bf16[4096,128]{1,0:T(8,128)(2,1)S(1)} fusion(bf16[8192,128]{1,0:T(8,128)(2,1)} %get-tuple-element.930, s32[4096]{0:T(1024)S(1)} %broadcast_clamp_fusion.4), kind=kCustom, calls=%fused_computation.clone.clone.1 | custom fusion | bytes 2113536 | tf_op jit(solution)/shard_map/while/body/eval_jaxpr/jit(_take)/gather | solution.py:21
  88.8 12.9 %gather_fusion = bf16[4096,128]{1,0:T(8,128)(2,1)S(1)} fusion(bf16[8192,128]{1,0:T(8,128)(2,1)} %get-tuple-element.930, s32[4096]{0:T(1024)S(1)} %broadcast_clamp_fusion.4), kind=kCustom, calls=%fused_computation.clone.clone.1 | custom fusion | bytes 2113536 | tf_op jit(solution)/shard_map/while/body/eval_jaxpr/jit(_take)/gather | solution.py:21
  106.6 12.9 %gather_fusion = bf16[4096,128]{1,0:T(8,128)(2,1)S(1)} fusion(bf16[8192,128]{1,0:T(8,128)(2,1)} %get-tuple-element.930, s32[4096]{0:T(1024)S(1)} %broadcast_clamp_fusion.4), kind=kCustom, calls=%fused_computation.clone.clone.1 | custom fusion | bytes 2113536 | tf_op jit(solution)/shard_map/while/body/eval_jaxpr/jit(_take)/gather | solution.py:21
  124.3 12.9 %gather_fusion = bf16[4096,128]{1,0:T(8,128)(2,1)S(1)} fusion(bf16[8192,128]{1,0:T(8,128)(2,1)} %get-tuple-element.930, s32[4096]{0:T(1024)S(1)} %broadcast_clamp_fusion.4), kind=kCustom, calls=%fused_computation.clone.clone.1 | custom fusion | bytes 2113536 | tf_op jit(solution)/shard_map/while/body/eval_jaxpr/jit(_take)/gather | solution.py:21
  142.0 12.9 %gather_fusion = bf16[4096,128]{1,0:T(8,128)(2,1)S(1)} fusion(bf16[8192,128]{1,0:T(8,128)(2,1)} %get-tuple-element.930, s32[4096]{0:T(1024)S(1)} %broadcast_clamp_fusion.4), kind=kCustom, calls=%fused_computation.clone.clone.1 | custom fusion | bytes 2113536 | tf_op jit(solution)/shard_map/while/body/eval_jaxpr/jit(_take)/gather | solution.py:21
  161.5 141.9 %while.62 = (s32[]{:T(128)}, bf16[8,512,128]{2,1,0:T(8,128)(2,1)}, s32[8,512]{1,0:T(8,128)S(1)}, s32[8,512,8]{2,1,0:T(8,128)}, bf16[8192,128]{1,0:T(8,128)(2,1)}, /*index=5*/s32[]{:T(128)}) while((s32[]{:T(128)}, bf16[8,512,128]{2,1,0:T(8,128)(2,1)}, s32[8,512]{1,0:T(8,128)S(1)}, s32[8,512,8]{2,1,0:T(8,128)}, bf16[8192,128]{1,0:T(8,128)(2,1)}, ...), condition=%wide.region_5.7_spmd, body=%wide.region_3.6_spmd.sunk | while | flops 2064386 | bytes 3676749 | solution.py:114
  162.8 12.9 %gather_fusion.1 = bf16[4096,128]{1,0:T(8,128)(2,1)S(1)} fusion(bf16[8192,128]{1,0:T(8,128)(2,1)} %get-tuple-element.912, s32[4096]{0:T(1024)S(1)} %broadcast_clamp_fusion.5), kind=kCustom, calls=%fused_computation.1.clone.clone.1 | custom fusion | bytes 2113536 | tf_op jit(solution)/shard_map/while/body/eval_jaxpr/jit(_take)/gather | solution.py:21
  180.5 12.9 %gather_fusion.1 = bf16[4096,128]{1,0:T(8,128)(2,1)S(1)} fusion(bf16[8192,128]{1,0:T(8,128)(2,1)} %get-tuple-element.912, s32[4096]{0:T(1024)S(1)} %broadcast_clamp_fusion.5), kind=kCustom, calls=%fused_computation.1.clone.clone.1 | custom fusion | bytes 2113536 | tf_op jit(solution)/shard_map/while/body/eval_jaxpr/jit(_take)/gather | solution.py:21
  198.3 12.9 %gather_fusion.1 = bf16[4096,128]{1,0:T(8,128)(2,1)S(1)} fusion(bf16[8192,128]{1,0:T(8,128)(2,1)} %get-tuple-element.912, s32[4096]{0:T(1024)S(1)} %broadcast_clamp_fusion.5), kind=kCustom, calls=%fused_computation.1.clone.clone.1 | custom fusion | bytes 2113536 | tf_op jit(solution)/shard_map/while/body/eval_jaxpr/jit(_take)/gather | solution.py:21
  216.0 12.9 %gather_fusion.1 = bf16[4096,128]{1,0:T(8,128)(2,1)S(1)} fusion(bf16[8192,128]{1,0:T(8,128)(2,1)} %get-tuple-element.912, s32[4096]{0:T(1024)S(1)} %broadcast_clamp_fusion.5), kind=kCustom, calls=%fused_computation.1.clone.clone.1 | custom fusion | bytes 2113536 | tf_op jit(solution)/shard_map/while/body/eval_jaxpr/jit(_take)/gather | solution.py:21
  233.8 12.9 %gather_fusion.1 = bf16[4096,128]{1,0:T(8,128)(2,1)S(1)} fusion(bf16[8192,128]{1,0:T(8,128)(2,1)} %get-tuple-element.912, s32[4096]{0:T(1024)S(1)} %broadcast_clamp_fusion.5), kind=kCustom, calls=%fused_computation.1.clone.clone.1 | custom fusion | bytes 2113536 | tf_op jit(solution)/shard_map/while/body/eval_jaxpr/jit(_take)/gather | solution.py:21
  251.5 12.9 %gather_fusion.1 = bf16[4096,128]{1,0:T(8,128)(2,1)S(1)} fusion(bf16[8192,128]{1,0:T(8,128)(2,1)} %get-tuple-element.912, s32[4096]{0:T(1024)S(1)} %broadcast_clamp_fusion.5), kind=kCustom, calls=%fused_computation.1.clone.clone.1 | custom fusion | bytes 2113536 | tf_op jit(solution)/shard_map/while/body/eval_jaxpr/jit(_take)/gather | solution.py:21
  269.3 12.9 %gather_fusion.1 = bf16[4096,128]{1,0:T(8,128)(2,1)S(1)} fusion(bf16[8192,128]{1,0:T(8,128)(2,1)} %get-tuple-element.912, s32[4096]{0:T(1024)S(1)} %broadcast_clamp_fusion.5), kind=kCustom, calls=%fused_computation.1.clone.clone.1 | custom fusion | bytes 2113536 | tf_op jit(solution)/shard_map/while/body/eval_jaxpr/jit(_take)/gather | solution.py:21
  287.0 12.9 %gather_fusion.1 = bf16[4096,128]{1,0:T(8,128)(2,1)S(1)} fusion(bf16[8192,128]{1,0:T(8,128)(2,1)} %get-tuple-element.912, s32[4096]{0:T(1024)S(1)} %broadcast_clamp_fusion.5), kind=kCustom, calls=%fused_computation.1.clone.clone.1 | custom fusion | bytes 2113536 | tf_op jit(solution)/shard_map/while/body/eval_jaxpr/jit(_take)/gather | solution.py:21
  306.6 6.5 %all-to-all-start = ((bf16[4,1024,2,128]{3,1,2,0:T(8,128)(2,1)}), bf16[4,1024,2,128]{3,1,2,0:T(8,128)(2,1)}, u32[]{:S(2)}, u32[]{:S(2)}) async-start(bf16[4,1024,2,128]{3,1,2,0:T(8,128)(2,1)} %copy.22), calls=%async_computation | async-start | bytes 4194304 | tf_op jit(solution)/shard_map/all_to_all | solution.py:122
  314.2 47.2 %all-to-all-done = bf16[4,1024,2,128]{3,1,2,0:T(8,128)(2,1)} async-done(((bf16[4,1024,2,128]{3,1,2,0:T(8,128)(2,1)}), bf16[4,1024,2,128]{3,1,2,0:T(8,128)(2,1)}, u32[]{:S(2)}, u32[]{:S(2)}) %all-to-all-start) | async-done | bytes 2097184 | tf_op jit(solution)/shard_map/all_to_all | solution.py:122
  373.1 44.5 %while.63 = (s32[]{:T(128)}, bf16[256,256]{1,0:T(8,128)(2,1)S(1)}, f32[1024]{0:T(1024)S(1)}, f32[1024]{0:T(1024)S(1)}, f32[1024]{0:T(1024)S(1)}, /*index=5*/s32[...) while((s32[]{:T(128)}, bf16[256,256]{1,0:T(8,128)(2,1)S(1)}, ...), condition=%wide.region_19.21_spmd, body=%wide.region_12.20_spmd.sunk | while | flops 136320288 | bytes 3772994 | solution.py:170
  373.4 5.0 collective-permute-done
  418.2 79.2 %while.64 = (s32[]{:T(128)}, bf16[256,256]{1,0:T(8,128)(2,1)}, f32[256,256]{1,0:T(8,128)S(1)}, f32[1024,256]{1,0:T(8,128)}, s32[]{:T(128)}, /*index=5*/s32[2,16]...) while((s32[]{:T(128)}, bf16[256,256]{1,0:T(8,128)(2,1)}, ...), condition=%wide.region_21.23_spmd.clone, body=%wide.region_20.22_spmd.clone.sunk | while | flops 405143840 | bytes 10253428 | solution.py:191
  498.1 18.1 %reduce-scatter.2.cloned.1.call-done = f32[64,256]{1,0:T(8,128)} async-done(((f32[256,256]{1,0:T(8,128)}), f32[64,256]{1,0:T(8,128)}) %reduce-scatter.2.cloned.1.call-update) | async-done | bytes 65552 | tf_op jit(solution)/shard_map/reduce_scatter | solution.py:195
  (411 shorter events, 224.2 us)
Async XLA Ops:
  306.6 54.7 %all-to-all-start = ((bf16[4,1024,2,128]{3,1,2,0:T(8,128)(2,1)}), bf16[4,1024,2,128]{3,1,2,0:T(8,128)(2,1)}, u32[]{:S(2)}, u32[]{:S(2)}) async-start(bf16[4,1024,2,128]{3,1,2,0:T(8,128)(2,1)} %copy.22), calls=%async_computation | async-start | bytes 4194304 | tf_op jit(solution)/shard_map/all_to_all | solution.py:122
  313.1 203.1 %reduce-scatter.2.cloned.1.call-start = ((), (), s32[]{:S(2)}) async-start(), calls=%async_computation.2 | async-start | bytes 327680 | tf_op jit(solution)/shard_map/reduce_scatter | solution.py:195
  373.1 5.3 %collective-permute-start = (bf16[256,256]{1,0:T(8,128)(2,1)S(1)}, bf16[256,256]{1,0:T(8,128)(2,1)S(1)}, u32[]{:S(2)}, u32[]{:S(2)}) collective-permute-start(bf16[256,256]{1,0:T(8,128)(2,1)S(1)} %get-tuple-element.950), channel_id=1, source_target_pairs={{0,4},{4,8},{8,12},{12,16},{16,20},{20,24},{24,28},{28,0},{1,5},{5... | collective-permute-start | bytes 393224 | tf_op jit(solution)/shard_map/while/body/eval_jaxpr/ppermute | solution.py:17
  379.4 5.3 %collective-permute-start = (bf16[256,256]{1,0:T(8,128)(2,1)S(1)}, bf16[256,256]{1,0:T(8,128)(2,1)S(1)}, u32[]{:S(2)}, u32[]{:S(2)}) collective-permute-start(bf16[256,256]{1,0:T(8,128)(2,1)S(1)} %get-tuple-element.950), channel_id=1, source_target_pairs={{0,4},{4,8},{8,12},{12,16},{16,20},{20,24},{24,28},{28,0},{1,5},{5... | collective-permute-start | bytes 393224 | tf_op jit(solution)/shard_map/while/body/eval_jaxpr/ppermute | solution.py:17
  385.8 5.3 %collective-permute-start = (bf16[256,256]{1,0:T(8,128)(2,1)S(1)}, bf16[256,256]{1,0:T(8,128)(2,1)S(1)}, u32[]{:S(2)}, u32[]{:S(2)}) collective-permute-start(bf16[256,256]{1,0:T(8,128)(2,1)S(1)} %get-tuple-element.950), channel_id=1, source_target_pairs={{0,4},{4,8},{8,12},{12,16},{16,20},{20,24},{24,28},{28,0},{1,5},{5... | collective-permute-start | bytes 393224 | tf_op jit(solution)/shard_map/while/body/eval_jaxpr/ppermute | solution.py:17
  392.1 5.3 %collective-permute-start = (bf16[256,256]{1,0:T(8,128)(2,1)S(1)}, bf16[256,256]{1,0:T(8,128)(2,1)S(1)}, u32[]{:S(2)}, u32[]{:S(2)}) collective-permute-start(bf16[256,256]{1,0:T(8,128)(2,1)S(1)} %get-tuple-element.950), channel_id=1, source_target_pairs={{0,4},{4,8},{8,12},{12,16},{16,20},{20,24},{24,28},{28,0},{1,5},{5... | collective-permute-start | bytes 393224 | tf_op jit(solution)/shard_map/while/body/eval_jaxpr/ppermute | solution.py:17
  404.8 5.3 %collective-permute-start = (bf16[256,256]{1,0:T(8,128)(2,1)S(1)}, bf16[256,256]{1,0:T(8,128)(2,1)S(1)}, u32[]{:S(2)}, u32[]{:S(2)}) collective-permute-start(bf16[256,256]{1,0:T(8,128)(2,1)S(1)} %get-tuple-element.950), channel_id=1, source_target_pairs={{0,4},{4,8},{8,12},{12,16},{16,20},{20,24},{24,28},{28,0},{1,5},{5... | collective-permute-start | bytes 393224 | tf_op jit(solution)/shard_map/while/body/eval_jaxpr/ppermute | solution.py:17
  411.2 5.3 %collective-permute-start = (bf16[256,256]{1,0:T(8,128)(2,1)S(1)}, bf16[256,256]{1,0:T(8,128)(2,1)S(1)}, u32[]{:S(2)}, u32[]{:S(2)}) collective-permute-start(bf16[256,256]{1,0:T(8,128)(2,1)S(1)} %get-tuple-element.950), channel_id=1, source_target_pairs={{0,4},{4,8},{8,12},{12,16},{16,20},{20,24},{24,28},{28,0},{1,5},{5... | collective-permute-start | bytes 393224 | tf_op jit(solution)/shard_map/while/body/eval_jaxpr/ppermute | solution.py:17
  419.1 5.5 %collective-permute-start.1 = (bf16[256,256]{1,0:T(8,128)(2,1)S(1)}, bf16[256,256]{1,0:T(8,128)(2,1)}, u32[]{:S(2)}, u32[]{:S(2)}) collective-permute-start(bf16[256,256]{1,0:T(8,128)(2,1)S(1)} %copy.58), channel_id=1, source_target_pairs={{0,4},{4,8},{8,12},{12,16},{16,20},{20,24},{24,28},{28,0},{1,5},{5... | collective-permute-start | bytes 393224 | tf_op jit(solution)/shard_map/while/body/eval_jaxpr/ppermute | solution.py:17
  421.2 6.9 %collective-permute-start.2 = (f32[256,256]{1,0:T(8,128)}, f32[256,256]{1,0:T(8,128)S(1)}, u32[]{:S(2)}, u32[]{:S(2)}) collective-permute-start(f32[256,256]{1,0:T(8,128)} %fusion.96), channel_id=1, source_target_pairs={{0,4},{4,8},{8,12},{12,16},{16,20},{20,24},{24,28},{28,0},{1,5},{5... | collective-permute-start | bytes 786440 | tf_op jit(solution)/shard_map/while/body/eval_jaxpr/ppermute | solution.py:17
  429.0 5.8 %collective-permute-start.1 = (bf16[256,256]{1,0:T(8,128)(2,1)S(1)}, bf16[256,256]{1,0:T(8,128)(2,1)}, u32[]{:S(2)}, u32[]{:S(2)}) collective-permute-start(bf16[256,256]{1,0:T(8,128)(2,1)S(1)} %copy.58), channel_id=1, source_target_pairs={{0,4},{4,8},{8,12},{12,16},{16,20},{20,24},{24,28},{28,0},{1,5},{5... | collective-permute-start | bytes 393224 | tf_op jit(solution)/shard_map/while/body/eval_jaxpr/ppermute | solution.py:17
  431.1 6.9 %collective-permute-start.2 = (f32[256,256]{1,0:T(8,128)}, f32[256,256]{1,0:T(8,128)S(1)}, u32[]{:S(2)}, u32[]{:S(2)}) collective-permute-start(f32[256,256]{1,0:T(8,128)} %fusion.96), channel_id=1, source_target_pairs={{0,4},{4,8},{8,12},{12,16},{16,20},{20,24},{24,28},{28,0},{1,5},{5... | collective-permute-start | bytes 786440 | tf_op jit(solution)/shard_map/while/body/eval_jaxpr/ppermute | solution.py:17
  438.9 5.9 %collective-permute-start.1 = (bf16[256,256]{1,0:T(8,128)(2,1)S(1)}, bf16[256,256]{1,0:T(8,128)(2,1)}, u32[]{:S(2)}, u32[]{:S(2)}) collective-permute-start(bf16[256,256]{1,0:T(8,128)(2,1)S(1)} %copy.58), channel_id=1, source_target_pairs={{0,4},{4,8},{8,12},{12,16},{16,20},{20,24},{24,28},{28,0},{1,5},{5... | collective-permute-start | bytes 393224 | tf_op jit(solution)/shard_map/while/body/eval_jaxpr/ppermute | solution.py:17
  441.0 6.9 %collective-permute-start.2 = (f32[256,256]{1,0:T(8,128)}, f32[256,256]{1,0:T(8,128)S(1)}, u32[]{:S(2)}, u32[]{:S(2)}) collective-permute-start(f32[256,256]{1,0:T(8,128)} %fusion.96), channel_id=1, source_target_pairs={{0,4},{4,8},{8,12},{12,16},{16,20},{20,24},{24,28},{28,0},{1,5},{5... | collective-permute-start | bytes 786440 | tf_op jit(solution)/shard_map/while/body/eval_jaxpr/ppermute | solution.py:17
  448.8 5.9 %collective-permute-start.1 = (bf16[256,256]{1,0:T(8,128)(2,1)S(1)}, bf16[256,256]{1,0:T(8,128)(2,1)}, u32[]{:S(2)}, u32[]{:S(2)}) collective-permute-start(bf16[256,256]{1,0:T(8,128)(2,1)S(1)} %copy.58), channel_id=1, source_target_pairs={{0,4},{4,8},{8,12},{12,16},{16,20},{20,24},{24,28},{28,0},{1,5},{5... | collective-permute-start | bytes 393224 | tf_op jit(solution)/shard_map/while/body/eval_jaxpr/ppermute | solution.py:17
  450.9 6.9 %collective-permute-start.2 = (f32[256,256]{1,0:T(8,128)}, f32[256,256]{1,0:T(8,128)S(1)}, u32[]{:S(2)}, u32[]{:S(2)}) collective-permute-start(f32[256,256]{1,0:T(8,128)} %fusion.96), channel_id=1, source_target_pairs={{0,4},{4,8},{8,12},{12,16},{16,20},{20,24},{24,28},{28,0},{1,5},{5... | collective-permute-start | bytes 786440 | tf_op jit(solution)/shard_map/while/body/eval_jaxpr/ppermute | solution.py:17
  458.7 5.9 %collective-permute-start.1 = (bf16[256,256]{1,0:T(8,128)(2,1)S(1)}, bf16[256,256]{1,0:T(8,128)(2,1)}, u32[]{:S(2)}, u32[]{:S(2)}) collective-permute-start(bf16[256,256]{1,0:T(8,128)(2,1)S(1)} %copy.58), channel_id=1, source_target_pairs={{0,4},{4,8},{8,12},{12,16},{16,20},{20,24},{24,28},{28,0},{1,5},{5... | collective-permute-start | bytes 393224 | tf_op jit(solution)/shard_map/while/body/eval_jaxpr/ppermute | solution.py:17
  460.7 6.9 %collective-permute-start.2 = (f32[256,256]{1,0:T(8,128)}, f32[256,256]{1,0:T(8,128)S(1)}, u32[]{:S(2)}, u32[]{:S(2)}) collective-permute-start(f32[256,256]{1,0:T(8,128)} %fusion.96), channel_id=1, source_target_pairs={{0,4},{4,8},{8,12},{12,16},{16,20},{20,24},{24,28},{28,0},{1,5},{5... | collective-permute-start | bytes 786440 | tf_op jit(solution)/shard_map/while/body/eval_jaxpr/ppermute | solution.py:17
  468.6 5.9 %collective-permute-start.1 = (bf16[256,256]{1,0:T(8,128)(2,1)S(1)}, bf16[256,256]{1,0:T(8,128)(2,1)}, u32[]{:S(2)}, u32[]{:S(2)}) collective-permute-start(bf16[256,256]{1,0:T(8,128)(2,1)S(1)} %copy.58), channel_id=1, source_target_pairs={{0,4},{4,8},{8,12},{12,16},{16,20},{20,24},{24,28},{28,0},{1,5},{5... | collective-permute-start | bytes 393224 | tf_op jit(solution)/shard_map/while/body/eval_jaxpr/ppermute | solution.py:17
  470.6 6.9 %collective-permute-start.2 = (f32[256,256]{1,0:T(8,128)}, f32[256,256]{1,0:T(8,128)S(1)}, u32[]{:S(2)}, u32[]{:S(2)}) collective-permute-start(f32[256,256]{1,0:T(8,128)} %fusion.96), channel_id=1, source_target_pairs={{0,4},{4,8},{8,12},{12,16},{16,20},{20,24},{24,28},{28,0},{1,5},{5... | collective-permute-start | bytes 786440 | tf_op jit(solution)/shard_map/while/body/eval_jaxpr/ppermute | solution.py:17
  478.5 5.9 %collective-permute-start.1 = (bf16[256,256]{1,0:T(8,128)(2,1)S(1)}, bf16[256,256]{1,0:T(8,128)(2,1)}, u32[]{:S(2)}, u32[]{:S(2)}) collective-permute-start(bf16[256,256]{1,0:T(8,128)(2,1)S(1)} %copy.58), channel_id=1, source_target_pairs={{0,4},{4,8},{8,12},{12,16},{16,20},{20,24},{24,28},{28,0},{1,5},{5... | collective-permute-start | bytes 393224 | tf_op jit(solution)/shard_map/while/body/eval_jaxpr/ppermute | solution.py:17
  480.5 6.9 %collective-permute-start.2 = (f32[256,256]{1,0:T(8,128)}, f32[256,256]{1,0:T(8,128)S(1)}, u32[]{:S(2)}, u32[]{:S(2)}) collective-permute-start(f32[256,256]{1,0:T(8,128)} %fusion.96), channel_id=1, source_target_pairs={{0,4},{4,8},{8,12},{12,16},{16,20},{20,24},{24,28},{28,0},{1,5},{5... | collective-permute-start | bytes 786440 | tf_op jit(solution)/shard_map/while/body/eval_jaxpr/ppermute | solution.py:17
  488.4 5.9 %collective-permute-start.1 = (bf16[256,256]{1,0:T(8,128)(2,1)S(1)}, bf16[256,256]{1,0:T(8,128)(2,1)}, u32[]{:S(2)}, u32[]{:S(2)}) collective-permute-start(bf16[256,256]{1,0:T(8,128)(2,1)S(1)} %copy.58), channel_id=1, source_target_pairs={{0,4},{4,8},{8,12},{12,16},{16,20},{20,24},{24,28},{28,0},{1,5},{5... | collective-permute-start | bytes 393224 | tf_op jit(solution)/shard_map/while/body/eval_jaxpr/ppermute | solution.py:17
  490.4 6.9 %collective-permute-start.2 = (f32[256,256]{1,0:T(8,128)}, f32[256,256]{1,0:T(8,128)S(1)}, u32[]{:S(2)}, u32[]{:S(2)}) collective-permute-start(f32[256,256]{1,0:T(8,128)} %fusion.96), channel_id=1, source_target_pairs={{0,4},{4,8},{8,12},{12,16},{16,20},{20,24},{24,28},{28,0},{1,5},{5... | collective-permute-start | bytes 786440 | tf_op jit(solution)/shard_map/while/body/eval_jaxpr/ppermute | solution.py:17
  (10 other events, 539.0 us)
Sparse Core Ops, SparseCore 0:
  498.2 17.8 reduce-scatter.1
where the time goes:
time: 525 us; the launch traced here: 523 us
  local copies, waits for them, and re-layouts  249 us (47%)
  waiting for transfers between devices  125 us (24%)
  other arithmetic  89.1 us (17%)
  matrix products  36.2 us (7%)
  between operations  14.2 us (3%)
  starting transfers between devices  7.37 us (1%)
    gather x16, local copies, waits for them, and re-layouts, pool_block(): gathered = jnp.take(table, block_ids, axis=0).astype(jnp.float32)  206 us
    ppermute x23, waiting for transfers between devices, shifted(): return lax.ppermute(value, axis, pairs)  60 us
    all_to_all x1, waiting for transfers between devices, local(): lax.all_to_all(pooled, 'tbl', split_axis=0, concat_axis=2, tiled=True)  47.2 us
    reduce_sum x16, other arithmetic, pool_block(): jnp.sum(jnp.where(in_bag[:, :, None], gathered, 0.0), axis=1)  45.9 us
    add x8, other arithmetic, lap_two(): user_grad = user_grad + user_term  19.6 us
    reduce_scatter x1, waiting for transfers between devices, local(): lax.psum_scatter(item_total, 'tbl', scatter_dimension=0, tiled=True)  18.1 us
    and x16, other arithmetic, pool_block(): gathered = jnp.take(table, block_ids, axis=0).astype(jnp.float32)  17.9 us
    dynamic_update_slice x16, local copies, waits for them, and re-layouts, local(): lax.map(lambda pair, table=table: pool_block(table, pair[0], pair[1]), (f...  10.7 us
  transfers between devices with their start and end apart: 25, of which 17 were waited for; matrix products, arithmetic and copies ran while one was open for 9% of the time, Pallas kernels for 0%

commit v1 on v0

v1 whole, which is shorter than its diff:
```python
import functools

import jax
import jax.numpy as jnp
from jax import lax
from jax.experimental import pallas as pl
from jax.experimental.pallas import tpu as pltpu
from jax.sharding import PartitionSpec as P

masked_value = -1e30
MIB = 1 << 20
MESH = pl.DeviceIdType.MESH


def pool_kernel(features, bag, ids_ref, table_ref, out_ref, sums_ref):
    users = out_ref.shape[0]
    width = table_ref.shape[2]

    def group(step, carry):
        first = pl.multiple_of(step * 8, 8)
        for user in range(8):
            for feature in range(features):
                rows = [
                    table_ref[ids_ref[(feature * bag + entry) * users + first + user]]
                    for entry in range(bag)
                ]
                while len(rows) > 1:
                    rows = [
                        rows[k] + rows[k + 1] if k + 1 < len(rows) else rows[k]
                        for k in range(0, len(rows), 2)
                    ]
                sums_ref[step, user : user + 1, feature * width : (feature + 1) * width] = rows[0]
        return carry

    lax.fori_loop(0, users // 8, group, 0)
    out_ref[...] = sums_ref[...].reshape(out_ref.shape).astype(out_ref.dtype)


def pool_chunk(ids, table, users, features, bag):
    width = table.shape[2]
    return pl.pallas_call(
        functools.partial(pool_kernel, features, bag),
        out_shape=jax.ShapeDtypeStruct((users, features * width), jnp.bfloat16),
        in_specs=[
            pl.BlockSpec(memory_space=pltpu.SMEM),
            pl.BlockSpec(memory_space=pltpu.VMEM),
        ],
        out_specs=pl.BlockSpec(memory_space=pltpu.VMEM),
        scratch_shapes=[pltpu.VMEM((users // 8, 8, features * width), jnp.float32)],
        compiler_params=pltpu.CompilerParams(vmem_limit_bytes=20 * MIB),
        cost_estimate=pl.CostEstimate(
            flops=users * features * bag * width * 100, bytes_accessed=16 * MIB, transcendentals=0
        ),
        name="pool_chunk",
    )(ids, table)


def main_kernel(
    order, me_ref, elig_ref, *refs
):
    count = len(order)
    piece_refs = refs[:count]
    (w1_ref, b1_ref, w2_ref, b2_ref, items_ref, pos_ref, loss_ref, ugrad_ref, igrad_ref,
     scores_ref, signal_ref, acc_ref) = refs[count:]
    tile = pl.program_id(0)
    tile_users = ugrad_ref.shape[0]
    items = items_ref.shape[0]
    blocks = elig_ref.shape[1]
    iblk = items // blocks
    user_block = tile * elig_ref.shape[0] // pl.num_programs(0)
    depth = piece_refs[0].shape[1]
    me = me_ref[0]

    hidden = None
    for position, distance in enumerate(order):
        source = lax.rem(me - distance + count, count)
        weight = w1_ref[pl.ds(pl.multiple_of(source * depth, depth), depth), :]
        part = jnp.dot(piece_refs[position][...], weight, preferred_element_type=jnp.float32)
        hidden = part if hidden is None else hidden + part
    hidden = jnp.maximum(hidden + b1_ref[...], 0.0).astype(jnp.bfloat16)
    queries = (
        jnp.dot(hidden, w2_ref[...], preferred_element_type=jnp.float32) + b2_ref[...]
    ).astype(jnp.bfloat16)

    wanted = pos_ref[...]
    row = lax.broadcasted_iota(jnp.int32, (iblk, tile_users), 0)
    peak = jnp.full((8, tile_users), masked_value, jnp.float32)
    chosen = jnp.zeros((8, tile_users), jnp.float32)
    for block in range(blocks):
        span = slice(block * iblk, (block + 1) * iblk)
        scores = lax.dot_general(
            items_ref[span, :], queries, (((1,), (1,)), ((), ())),
            preferred_element_type=jnp.float32,
        )
        scores = jnp.where(elig_ref[user_block, block] > 0, scores, masked_value)
        target = row == wanted - block * iblk
        chosen += jnp.sum(
            jnp.where(target, scores, 0.0).reshape(iblk // 8, 8, tile_users), axis=0
        )
        peak = jnp.maximum(peak, jnp.max(scores.reshape(iblk // 8, 8, tile_users), axis=0))
        scores_ref[span, :] = scores
    peak = jnp.max(peak, axis=0, keepdims=True)
    chosen = jnp.sum(chosen, axis=0, keepdims=True)
    total = jnp.zeros((8, tile_users), jnp.float32)
    for block in range(blocks):
        span = slice(block * iblk, (block + 1) * iblk)
        weights = jnp.exp(scores_ref[span, :] - peak)
        total += jnp.sum(weights.reshape(iblk // 8, 8, tile_users), axis=0)
        scores_ref[span, :] = weights
    total = jnp.sum(total, axis=0, keepdims=True)
    loss_ref[...] = peak + jnp.log(total) - chosen
    inverse = 1.0 / total
    for block in range(blocks):
        span = slice(block * iblk, (block + 1) * iblk)
        target = row == wanted - block * iblk
        signal_ref[span, :] = (
            scores_ref[span, :] * inverse - target.astype(jnp.float32)
        ).astype(jnp.bfloat16)
    ugrad_ref[...] = lax.dot_general(
        signal_ref[...], items_ref[...], (((0,), (0,)), ((), ())),
        preferred_element_type=jnp.float32,
    )
    part = jnp.dot(signal_ref[...], queries, preferred_element_type=jnp.float32)

    @pl.when(tile == 0)
    def _():
        acc_ref[...] = part

    @pl.when(tile > 0)
    def _():
        acc_ref[...] += part

    @pl.when(tile == pl.num_programs(0) - 1)
    def _():
        igrad_ref[...] = acc_ref[...].astype(igrad_ref.dtype)


def main_call(order, me, pieces, w_hidden, b_hidden, w_out, b_out, items, elig, positives):
    users, depth = pieces[0].shape
    tile_users = 256
    tiles = users // tile_users
    count, width = items.shape
    hid = w_hidden.shape[1]
    whole = lambda shape: pl.BlockSpec(shape, lambda i: (0, 0))
    smem = pl.BlockSpec(memory_space=pltpu.SMEM)
    return pl.pallas_call(
        functools.partial(main_kernel, order),
        grid=(tiles,),
        out_shape=(
            jax.ShapeDtypeStruct((1, users), jnp.float32),
            jax.ShapeDtypeStruct((users, width), jnp.float32),
            jax.ShapeDtypeStruct((count, width), jnp.bfloat16),
        ),
        in_specs=[smem, smem]
        + [pl.BlockSpec((tile_users, depth), lambda i: (i, 0))] * len(order)
        + [
            whole(w_hidden.shape),
            whole((1, hid)),
            whole(w_out.shape),
            whole((1, width)),
            whole((count, width)),
            pl.BlockSpec((1, tile_users), lambda i: (0, i)),
        ],
        out_specs=(
            pl.BlockSpec((1, tile_users), lambda i: (0, i)),
            pl.BlockSpec((tile_users, width), lambda i: (i, 0)),
            whole((count, width)),
        ),
        scratch_shapes=[
            pltpu.VMEM((count, tile_users), jnp.float32),
            pltpu.VMEM((count, tile_users), jnp.bfloat16),
            pltpu.VMEM((count, width), jnp.float32),
        ],
        compiler_params=pltpu.CompilerParams(vmem_limit_bytes=48 * MIB),
        name="tower_and_softmax",
    )(
        me, elig, *pieces, w_hidden, b_hidden.reshape(1, hid), w_out, b_out.reshape(1, width),
        items, positives.reshape(1, users),
    )


def reduce_kernel(
    chips, shards, part_ref, out_ref, got_a, sum_a, got_b, sum_b, got_c,
    send_a, recv_a, send_b, recv_b, send_c, recv_c,
):
    item = lax.axis_index("item")
    shard = lax.axis_index("tbl")
    core = lax.rem(item, 2)
    chip = item // 2
    other_core = (2 * chip + 1 - core, shard)
    chip_at = lambda k: (2 * lax.rem(chip + k, chips) + core, shard)
    shard_at = lambda k: (item, lax.rem(shard + k, shards))
    partners = (
        [other_core]
        + [chip_at(k) for k in range(1, chips)]
        + [shard_at(k) for k in range(1, shards)]
    )
    barrier = pltpu.get_barrier_semaphore()
    for partner in partners:
        pl.semaphore_signal(barrier, inc=1, device_id=partner, device_id_type=MESH)
    pl.semaphore_wait(barrier, len(partners))

    copy = pltpu.make_async_remote_copy(
        src_ref=part_ref.at[:, 1 - core], dst_ref=got_a, send_sem=send_a, recv_sem=recv_a,
        device_id=other_core, device_id_type=MESH,
    )
    copy.start()
    copy.wait()
    sum_a[...] = (
        part_ref[:, core].astype(jnp.float32) + got_a[...].astype(jnp.float32)
    ).astype(sum_a.dtype)

    copies = []
    for k in range(1, chips):
        copies.append(pltpu.make_async_remote_copy(
            src_ref=sum_a.at[lax.rem(chip + k, chips)], dst_ref=got_b.at[k - 1],
            send_sem=send_b.at[k - 1], recv_sem=recv_b.at[k - 1],
            device_id=chip_at(k), device_id_type=MESH,
        ))
        copies[-1].start()
    total = sum_a[chip].astype(jnp.float32)
    for k in range(1, chips):
        copies[k - 1].wait()
        total += got_b[k - 1].astype(jnp.float32)
    rows = out_ref.shape[0]
    sum_b[...] = total.astype(sum_b.dtype).reshape(shards, rows, total.shape[1])

    copies = []
    for k in range(1, shards):
        copies.append(pltpu.make_async_remote_copy(
            src_ref=sum_b.at[lax.rem(shard + k, shards)], dst_ref=got_c.at[k - 1],
            send_sem=send_c.at[k - 1], recv_sem=recv_c.at[k - 1],
            device_id=shard_at(k), device_id_type=MESH,
        ))
        copies[-1].start()
    total = sum_b[shard].astype(jnp.float32)
    for k in range(1, shards):
        copies[k - 1].wait()
        total += got_c[k - 1].astype(jnp.float32)
    out_ref[...] = total


def reduce_call(partial):
    chips, _, rows, width = partial.shape
    shards = lax.axis_size("tbl")
    piece = rows // shards
    dma = pltpu.SemaphoreType.DMA
    return pl.pallas_call(
        functools.partial(reduce_kernel, chips, shards),
        out_shape=jax.ShapeDtypeStruct((piece, width), jnp.float32),
        in_specs=[pl.BlockSpec(memory_space=pltpu.VMEM)],
        out_specs=pl.BlockSpec(memory_space=pltpu.VMEM),
        scratch_shapes=[
            pltpu.VMEM((chips, rows, width), jnp.bfloat16),
            pltpu.VMEM((chips, rows, width), jnp.bfloat16),
            pltpu.VMEM((chips - 1, rows, width), jnp.bfloat16),
            pltpu.VMEM((shards, piece, width), jnp.bfloat16),
            pltpu.VMEM((shards - 1, piece, width), jnp.bfloat16),
            dma, dma,
            dma((chips - 1,)), dma((chips - 1,)),
            dma((shards - 1,)), dma((shards - 1,)),
        ],
        compiler_params=pltpu.CompilerParams(
            collective_id=0, has_side_effects=True, vmem_limit_bytes=24 * MIB
        ),
        name="reduce_item_grad",
    )(partial)


def local(
    tables, feat_ids, bag_lens, w_hidden, b_hidden, w_out, b_out, item_vecs, elig_mask, positives
):
    shards = lax.axis_size("tbl")
    me = lax.axis_index("tbl")
    group_users, features, bag = feat_ids.shape
    users = group_users // shards
    rows, width = tables.shape[1:]

    items = lax.all_gather(item_vecs, "item", axis=0, tiled=True)

    zero_row = features * rows
    table = jnp.concatenate(
        [
            tables.astype(jnp.float32).reshape(zero_row, 1, width),
            jnp.zeros((8, 1, width), jnp.float32),
        ]
    )
    ids = jnp.transpose(feat_ids, (1, 2, 0))
    lens = jnp.transpose(bag_lens, (1, 0))
    in_bag = jnp.arange(bag, dtype=jnp.int32)[None, :, None] < lens[:, None, :]
    base = (jnp.arange(features, dtype=jnp.int32) * rows)[:, None, None]
    ids = jnp.where(in_bag, ids + base, zero_row)
    ids = jnp.transpose(ids.reshape(features * bag, shards, users), (1, 0, 2))
    ids = ids.reshape(shards, features * bag * users)

    order = sorted(range(1, shards), key=lambda d: (abs(2 * d - shards), d)) + [0]
    pieces = []
    for distance in order:
        target = lax.rem(me + distance, shards)
        chunk = lax.dynamic_index_in_dim(ids, target, 0, keepdims=False)
        pooled = pool_chunk(chunk, table, users, features, bag)
        if distance:
            pairs = [(source, (source + distance) % shards) for source in range(shards)]
            pooled = lax.ppermute(pooled, "tbl", pairs)
        pieces.append(pooled)

    loss, user_grad, partial = main_call(
        tuple(order), me.reshape(1).astype(jnp.int32), pieces, w_hidden, b_hidden, w_out, b_out,
        items, elig_mask, positives,
    )
    cycle = lax.axis_size("item")
    partial = partial.reshape(cycle // 2, 2, item_vecs.shape[0], item_vecs.shape[1])
    item_grad = reduce_call(partial)
    return (loss.reshape(users), user_grad, item_grad)


def solution(mesh):
    in_specs = (
        P("tbl", None, None),
        P("item", "tbl", None),
        P("item", "tbl"),
        P(),
        P(),
        P(),
        P(),
        P("item", None),
        P(("item", "tbl"), None),
        P(("item", "tbl")),
    )
    out_specs = (P(("item", "tbl")), P(("item", "tbl"), None), P(("item", "tbl"), None))
    return jax.shard_map(local, mesh=mesh, in_specs=in_specs, out_specs=out_specs, check_vma=False)
```

time: 525 us -> 138 us (0.26)
  local copies, waits for them, and re-layouts: 249 us -> 10 us
  waiting for transfers between devices: 125 us -> 0.71 us
  Pallas kernels: 0 us -> 94 us
  other arithmetic: 89.1 us -> 10.4 us
  matrix products: 36.2 us -> 0 us
    gather x16 -> x0, local copies, waits for them, and re-layouts: 206 us -> none  [pool_block(): gathered = jnp.take(table, block_ids, axis=0).astype(jnp.float32)]
    pallas_call x0 -> x6, Pallas kernels: none -> 94 us  [the longest x4 61.9 us: pool_chunk(): pl.pallas_call(functools.partial(pool_kernel, features, bag), out_shape=j...]
    ppermute x23 -> x3, waiting for transfers between devices: 60 us -> 0.01 us  [local(): pooled = lax.ppermute(pooled, 'tbl', pairs)]
    reduce_sum x24 -> x0, other arithmetic: 48.6 us -> none  [the longest x16 45.9 us: pool_block(): jnp.sum(jnp.where(in_bag[:, :, None], gathered, 0.0), axis=1)]
    all_to_all x1 -> x0, waiting for transfers between devices: 47.2 us -> none  [local(): lax.all_to_all(pooled, 'tbl', split_axis=0, concat_axis=2, tiled=True)]
    dot_general x65 -> x0, matrix products: 36.2 us -> none  [the longest x16 9.99 us: contribute(): jnp.einsum('ui,id->ud', signal, visiting, preferred_element_type=jnp.floa...]
    add x33 -> x0, other arithmetic: 19.8 us -> none  [the longest x8 19.6 us: lap_two(): user_grad = user_grad + user_term]
    reduce_scatter x1 -> x0, waiting for transfers between devices: 18.1 us -> none  [local(): lax.psum_scatter(item_total, 'tbl', scatter_dimension=0, tiled=True)]
  transfers between devices with their start and end apart: 25 -> 4, of which waited for: 17 -> 0; matrix products, arithmetic and copies ran while one was open for 9% -> 13% of each run, Pallas kernels for 0% -> 45%
where the time goes in v1:
time: 138 us; the launch traced here: 137 us
  Pallas kernels  94 us (68%)
  between operations  14.2 us (10%)
  other arithmetic  10.4 us (8%)
  local copies, waits for them, and re-layouts  10 us (7%)
  starting transfers between devices  8.07 us (6%)
    pallas_call x4, Pallas kernels, pool_chunk(): pl.pallas_call(functools.partial(pool_kernel, features, bag), out_shape=j...  61.9 us
    pallas_call x1, Pallas kernels, reduce_call(): pl.pallas_call(functools.partial(reduce_kernel, chips, shards), out_shape...  16.1 us
    pallas_call x1, Pallas kernels, main_call(): pl.pallas_call(functools.partial(main_kernel, order), grid=(tiles,), out_...  16 us
    concatenate x1, other arithmetic, local(): jnp.concatenate([tables.astype(jnp.float32).reshape(zero_row, 1, width),...  9.31 us
    ppermute x3, starting transfers between devices, local(): pooled = lax.ppermute(pooled, 'tbl', pairs)  8.03 us
    reshape x1, local copies, waits for them, and re-layouts, local(): tables.astype(jnp.float32).reshape(zero_row, 1, width)  7.75 us
  transfers between devices with their start and end apart: 4, of which 0 were waited for; matrix products, arithmetic and copies ran while one was open for 13% of the time, Pallas kernels for 45%

profile of v1, /device:TPU:0, one launch (start us, length us, event | category | flops | bytes accessed | tf_op | source)
XLA Modules:
  0.0 137.4 jit_solution(7851745299202613461)
XLA Ops:
  7.2 0.0 all-gather.2.cloned.1.call-start
  7.2 0.7 all-gather.2.cloned.1.call-update
  7.9 1.0 bitcast_select_fusion
  9.0 0.2 reshape.40
  9.2 0.2 constant_dynamic-slice_fusion
  9.4 7.8 %copy.13 = bf16[16384,1,128]{2,1,0:T(2,128)(2,1)S(1)} copy(bf16[16384,1,128]{2,0,1:T(8,128)(2,1)} %bitcast.25) | data formatting | bytes 8388608 | tf_op jit(solution)/shard_map/reshape | solution.py:284
  17.2 9.3 %pad_convert_fusion.table_ref = f32[16392,1,128]{2,1,0:T(1,128)S(1)} fusion(bf16[16384,1,128]{2,1,0:T(2,128)(2,1)S(1)} %copy.13), kind=kLoop, calls=%fused_computation | loop fusion | flops 2098176 | bytes 12587008 | tf_op jit(solution)/shard_map/concatenate | solution.py:282
  26.5 15.5 %pool_chunk.4 = bf16[1024,256]{1,0:T(8,128)(2,1)S(1)} custom-call(s32[16384]{0:T(1024)S(1)} %bitcast.21, f32[16392,1,128]{2,1,0:T(1,128)S(1)} %pad_convert_fusion.table_ref), custom_call_target="tpu_custom_call" | custom-call | flops 209715200 | bytes 16777216 | tf_op jit(solution)/shard_map/pool_chunk/pallas_call | solution.py:41
  42.0 4.1 %collective-permute-start = (bf16[1024,256]{1,0:T(8,128)(2,1)S(1)}, bf16[1024,256]{1,0:T(8,128)(2,1)S(1)}, u32[]{:S(2)}, u32[]{:S(2)}) collective-permute-start(bf16[1024,256]{1,0:T(8,128)(2,1)S(1)} %pool_chunk.4), channel_id=1, source_target_pairs={{0,2},{1,3},{2,0},{3,1},{4,6},{5,7},{6,4},{7,5},{8,10},{9,11},{10,... | collective-permute-start | bytes 1572872 | tf_op jit(solution)/shard_map/ppermute | solution.py:304
  46.1 15.5 %pool_chunk.5 = bf16[1024,256]{1,0:T(8,128)(2,1)S(1)} custom-call(s32[16384]{0:T(1024)S(1)} %bitcast.20, f32[16392,1,128]{2,1,0:T(1,128)S(1)} %pad_convert_fusion.table_ref), custom_call_target="tpu_custom_call" | custom-call | flops 209715200 | bytes 16777216 | tf_op jit(solution)/shard_map/pool_chunk/pallas_call | solution.py:41
  61.6 1.6 %collective-permute-start.1 = (bf16[1024,256]{1,0:T(8,128)(2,1)S(1)}, bf16[1024,256]{1,0:T(8,128)(2,1)S(1)}, u32[]{:S(2)}, u32[]{:S(2)}) collective-permute-start(bf16[1024,256]{1,0:T(8,128)(2,1)S(1)} %pool_chunk.5), channel_id=1, source_target_pairs={{0,1},{1,2},{2,3},{3,0},{4,5},{5,6},{6,7},{7,4},{8,9},{9,10},{10,1... | collective-permute-start | bytes 1572872 | tf_op jit(solution)/shard_map/ppermute | solution.py:304
  63.2 0.0 copy-start.5
  63.2 15.5 %pool_chunk.6 = bf16[1024,256]{1,0:T(8,128)(2,1)S(1)} custom-call(s32[16384]{0:T(1024)S(1)} %bitcast.19, f32[16392,1,128]{2,1,0:T(1,128)S(1)} %pad_convert_fusion.table_ref), custom_call_target="tpu_custom_call" | custom-call | flops 209715200 | bytes 16777216 | tf_op jit(solution)/shard_map/pool_chunk/pallas_call | solution.py:41
  78.7 2.3 %collective-permute-start.2 = (bf16[1024,256]{1,0:T(8,128)(2,1)S(1)}, bf16[1024,256]{1,0:T(8,128)(2,1)S(1)}, u32[]{:S(2)}, u32[]{:S(2)}) collective-permute-start(bf16[1024,256]{1,0:T(8,128)(2,1)S(1)} %pool_chunk.6), channel_id=1, source_target_pairs={{0,3},{1,0},{2,1},{3,2},{4,7},{5,4},{6,5},{7,6},{8,11},{9,8},{10,9... | collective-permute-start | bytes 1572872 | tf_op jit(solution)/shard_map/ppermute | solution.py:304
  81.0 15.5 %pool_chunk.7.refs_3_ = bf16[1024,256]{1,0:T(8,128)(2,1)S(1)} custom-call(s32[16384]{0:T(1024)S(1)} %bitcast.18, f32[16392,1,128]{2,1,0:T(1,128)S(1)} %pad_convert_fusion.table_ref), custom_call_target="tpu_custom_call" | custom-call | flops 209715200 | bytes 16777216 | tf_op jit(solution)/shard_map/pool_chunk/pallas_call | solution.py:41
  96.5 0.0 collective-permute-done.refs_0_
  96.5 0.0 collective-permute-done.1.refs_1_
  96.5 0.0 collective-permute-done.2.refs_2_
  96.5 0.0 all-gather.2.cloned.1.call-done.refs_8_
  96.5 0.0 copy-done.1
  96.6 1.2 copy-done
  97.8 16.0 %tower_and_softmax.1 = (f32[1,1024]{1,0:T(1,128)}, f32[1024,256]{1,0:T(8,128)}, bf16[2048,256]{1,0:T(8,128)(2,1)S(1)}) custom-call(s32[1]{0:T(128)} %bitcast.me_ref, s32[2,16]{1,0:T(2,128)S(1)} %copy-done.4, bf16[1024,256]{1,0:T(8,128)(2,1)S(1)} %collective-permute-done.refs_0_, bf16[1024,256]{1,0:T(8,128)(2,1)S(1)} %collective-permute-done.1.refs_1_, ...), custom_call_target="tpu_custom_call" | custom-call | tf_op jit(solution)/shard_map/tower_and_softmax/pallas_call | solution.py:146
  113.9 16.1 %reduce_item_grad.1 = f32[64,256]{1,0:T(8,128)S(1)} custom-call(bf16[4,2,256,256]{3,2,1,0:T(8,128)(2,1)S(1)} %bitcast.17), custom_call_target="tpu_custom_call" | custom-call | tf_op jit(solution)/shard_map/reduce_item_grad/pallas_call | solution.py:248
  130.0 0.6 copy.15
  (10 shorter events, 0.0 us)
Async XLA Ops:
  7.2 89.4 %all-gather.2.cloned.1.call-start = ((), (), s32[]{:S(2)}) async-start(), calls=%async_computation | async-start | bytes 1179648 | tf_op jit(solution)/shard_map/all_gather | solution.py:279
  42.0 54.5 %collective-permute-start = (bf16[1024,256]{1,0:T(8,128)(2,1)S(1)}, bf16[1024,256]{1,0:T(8,128)(2,1)S(1)}, u32[]{:S(2)}, u32[]{:S(2)}) collective-permute-start(bf16[1024,256]{1,0:T(8,128)(2,1)S(1)} %pool_chunk.4), channel_id=1, source_target_pairs={{0,2},{1,3},{2,0},{3,1},{4,6},{5,7},{6,4},{7,5},{8,10},{9,11},{10,... | collective-permute-start | bytes 1572872 | tf_op jit(solution)/shard_map/ppermute | solution.py:304
  61.6 34.9 %collective-permute-start.1 = (bf16[1024,256]{1,0:T(8,128)(2,1)S(1)}, bf16[1024,256]{1,0:T(8,128)(2,1)S(1)}, u32[]{:S(2)}, u32[]{:S(2)}) collective-permute-start(bf16[1024,256]{1,0:T(8,128)(2,1)S(1)} %pool_chunk.5), channel_id=1, source_target_pairs={{0,1},{1,2},{2,3},{3,0},{4,5},{5,6},{6,7},{7,4},{8,9},{9,10},{10,1... | collective-permute-start | bytes 1572872 | tf_op jit(solution)/shard_map/ppermute | solution.py:304
  63.2 33.3 %copy-start.1 = (bf16[1024,256]{1,0:T(8,128)(2,1)S(1)}, bf16[1024,256]{1,0:T(8,128)(2,1)}, u32[]{:S(2)}) copy-start(bf16[1024,256]{1,0:T(8,128)(2,1)} %refs_6_.1) | copy-start | bytes 1572868
  63.2 33.4 %copy-start.2 = (f32[1024]{0:T(1024)S(1)}, f32[1024]{0:T(1024)}, u32[]{:S(2)}) copy-start(f32[1024]{0:T(1024)} %param.14) | copy-start | bytes 12292
  63.2 33.4 %copy-start.3 = (s32[1024]{0:T(1024)S(1)}, s32[1024]{0:T(1024)}, u32[]{:S(2)}) copy-start(s32[1024]{0:T(1024)} %param.19) | copy-start | bytes 12292
  63.2 33.4 %copy-start.4 = (s32[2,16]{1,0:T(2,128)S(1)}, s32[2,16]{1,0:T(2,128)}, u32[]{:S(2)}) copy-start(s32[2,16]{1,0:T(2,128)} %elig_ref.1) | copy-start | bytes 388
  63.2 33.4 %copy-start.5 = (f32[256]{0:T(256)S(1)}, f32[256]{0:T(256)}, u32[]{:S(2)}) copy-start(f32[256]{0:T(256)} %param.16) | copy-start | bytes 3076
  78.7 17.8 %collective-permute-start.2 = (bf16[1024,256]{1,0:T(8,128)(2,1)S(1)}, bf16[1024,256]{1,0:T(8,128)(2,1)S(1)}, u32[]{:S(2)}, u32[]{:S(2)}) collective-permute-start(bf16[1024,256]{1,0:T(8,128)(2,1)S(1)} %pool_chunk.6), channel_id=1, source_target_pairs={{0,3},{1,0},{2,1},{3,2},{4,7},{5,4},{6,5},{7,6},{8,11},{9,8},{10,9... | collective-permute-start | bytes 1572872 | tf_op jit(solution)/shard_map/ppermute | solution.py:304
  96.6 1.2 copy-start
Sparse Core Ops, SparseCore 0:
  9.9 26.1 all-gather.1

commit v2 on v1

--- a/solution.py
+++ b/solution.py
@@ -21,7 +21,7 @@
         for user in range(8):
             for feature in range(features):
                 rows = [
-                    table_ref[ids_ref[(feature * bag + entry) * users + first + user]]
+                    table_ref[ids_ref[first + ((feature * bag + entry) * users + user)]]
                     for entry in range(bag)
                 ]
                 while len(rows) > 1:
@@ -55,13 +55,11 @@
     )(ids, table)
 
 
-def main_kernel(
-    order, me_ref, elig_ref, *refs
-):
+def main_kernel(order, owned, me_ref, elig_ref, *refs):
     count = len(order)
     piece_refs = refs[:count]
-    (w1_ref, b1_ref, w2_ref, b2_ref, items_ref, pos_ref, loss_ref, ugrad_ref, igrad_ref,
-     scores_ref, signal_ref, acc_ref) = refs[count:]
+    (w1_ref, b1_ref, w2_ref, b2_ref, mixed_ref, pos_ref, loss_ref, ugrad_ref, igrad_ref,
+     items_ref, scores_ref, signal_ref, acc_ref) = refs[count:]
     tile = pl.program_id(0)
     tile_users = ugrad_ref.shape[0]
     items = items_ref.shape[0]
@@ -70,6 +68,12 @@
     user_block = tile * elig_ref.shape[0] // pl.num_programs(0)
     depth = piece_refs[0].shape[1]
     me = me_ref[0]
+
+    @pl.when(tile == 0)
+    def _():
+        for owner in range(items // owned):
+            place = pl.multiple_of((me_ref[1] ^ owner) * owned, owned)
+            items_ref[owner * owned : (owner + 1) * owned, :] = mixed_ref[pl.ds(place, owned), :]
 
     hidden = None
     for position, distance in enumerate(order):
@@ -135,7 +139,7 @@
         igrad_ref[...] = acc_ref[...].astype(igrad_ref.dtype)
 
 
-def main_call(order, me, pieces, w_hidden, b_hidden, w_out, b_out, items, elig, positives):
+def main_call(order, owned, me, pieces, w_hidden, b_hidden, w_out, b_out, items, elig, positives):
     users, depth = pieces[0].shape
     tile_users = 256
     tiles = users // tile_users
@@ -144,7 +148,7 @@
     whole = lambda shape: pl.BlockSpec(shape, lambda i: (0, 0))
     smem = pl.BlockSpec(memory_space=pltpu.SMEM)
     return pl.pallas_call(
-        functools.partial(main_kernel, order),
+        functools.partial(main_kernel, order, owned),
         grid=(tiles,),
         out_shape=(
             jax.ShapeDtypeStruct((1, users), jnp.float32),
@@ -167,6 +171,7 @@
             whole((count, width)),
         ),
         scratch_shapes=[
+            pltpu.VMEM((count, width), jnp.bfloat16),
             pltpu.VMEM((count, tile_users), jnp.float32),
             pltpu.VMEM((count, tile_users), jnp.bfloat16),
             pltpu.VMEM((count, width), jnp.float32),
@@ -276,15 +281,17 @@
     users = group_users // shards
     rows, width = tables.shape[1:]
 
-    items = lax.all_gather(item_vecs, "item", axis=0, tiled=True)
+    cycle = lax.axis_size("item")
+    items = item_vecs
+    reach = 1
+    while reach < cycle:
+        pairs = [(source, source ^ reach) for source in range(cycle)]
+        items = jnp.concatenate([items, lax.ppermute(items, "item", pairs)])
+        reach *= 2
 
     zero_row = features * rows
-    table = jnp.concatenate(
-        [
-            tables.astype(jnp.float32).reshape(zero_row, 1, width),
-            jnp.zeros((8, 1, width), jnp.float32),
-        ]
-    )
+    table = jnp.pad(tables.reshape(zero_row, width).astype(jnp.float32), ((0, 8), (0, 0)))
+    table = lax.optimization_barrier(table).reshape(zero_row + 8, 1, width)
     ids = jnp.transpose(feat_ids, (1, 2, 0))
     lens = jnp.transpose(bag_lens, (1, 0))
     in_bag = jnp.arange(bag, dtype=jnp.int32)[None, :, None] < lens[:, None, :]
@@ -305,10 +312,10 @@
         pieces.append(pooled)
 
     loss, user_grad, partial = main_call(
-        tuple(order), me.reshape(1).astype(jnp.int32), pieces, w_hidden, b_hidden, w_out, b_out,
+        tuple(order), item_vecs.shape[0],
+        jnp.stack([me, lax.axis_index("item")]).astype(jnp.int32), pieces, w_hidden, b_hidden, w_out, b_out,
         items, elig_mask, positives,
     )
-    cycle = lax.axis_size("item")
     partial = partial.reshape(cycle // 2, 2, item_vecs.shape[0], item_vecs.shape[1])
     item_grad = reduce_call(partial)
     return (loss.reshape(users), user_grad, item_grad)

time: 138 us -> 129 us (0.935)
  between operations: 14.2 us -> 0.88 us
  waiting for transfers between devices: 0.71 us -> 6.62 us
  starting transfers between devices: 8.07 us -> 11.5 us
  other arithmetic: 10.4 us -> 8.06 us
  local copies, waits for them, and re-layouts: 10 us -> 7.85 us
    reshape x1 -> x0, local copies, waits for them, and re-layouts: 7.75 us -> none  [local(): tables.astype(jnp.float32).reshape(zero_row, 1, width)]
    concatenate x1 -> x3, other arithmetic: 9.31 us -> 2.08 us  [local(): items = jnp.concatenate([items, lax.ppermute(items, 'item', pairs)])]
    ppermute x0 -> x3, waiting for transfers between devices: none -> 6.61 us  [local(): items = jnp.concatenate([items, lax.ppermute(items, 'item', pairs)])]
    pad x0 -> x1, other arithmetic: none -> 5.8 us  [local(): jnp.pad(tables.reshape(zero_row, width).astype(jnp.float32), ((0, 8), (0,...]
    unnamed x13 -> x27, local copies, waits for them, and re-layouts: 1.87 us -> 7.44 us
    ppermute x0 -> x3, starting transfers between devices: none -> 4.88 us  [local(): items = jnp.concatenate([items, lax.ppermute(items, 'item', pairs)])]
    ppermute x3, starting transfers between devices: 8.03 us -> 6.58 us  [local(): pooled = lax.ppermute(pooled, 'tbl', pairs)]
  transfers between devices with their start and end apart: 4 -> 6, of which waited for: 0 -> 1; matrix products, arithmetic and copies ran while one was open for 13% -> 6% of each run, Pallas kernels for 45% -> 48%
where the time goes in v2:
time: 129 us
  Pallas kernels  94.2 us (73%)
  starting transfers between devices  11.5 us (9%)
  other arithmetic  8.06 us (6%)
  local copies, waits for them, and re-layouts  7.85 us (6%)
  waiting for transfers between devices  6.62 us (5%)
    pallas_call x4, Pallas kernels, pool_chunk(): pl.pallas_call(functools.partial(pool_kernel, features, bag), out_shape=j...  61.9 us
    pallas_call x1, Pallas kernels, main_call(): pl.pallas_call(functools.partial(main_kernel, order, owned), grid=(tiles,...  16.2 us
    pallas_call x1, Pallas kernels, reduce_call(): pl.pallas_call(functools.partial(reduce_kernel, chips, shards), out_shape...  16.1 us
    unnamed x27, local copies, waits for them, and re-layouts  7.44 us
    ppermute x3, waiting for transfers between devices, local(): items = jnp.concatenate([items, lax.ppermute(items, 'item', pairs)])  6.61 us
    ppermute x3, starting transfers between devices, local(): pooled = lax.ppermute(pooled, 'tbl', pairs)  6.58 us
    pad x1, other arithmetic, local(): jnp.pad(tables.reshape(zero_row, width).astype(jnp.float32), ((0, 8), (0,...  5.8 us
    ppermute x3, starting transfers between devices, local(): items = jnp.concatenate([items, lax.ppermute(items, 'item', pairs)])  4.88 us
  transfers between devices with their start and end apart: 6, of which 1 were waited for; matrix products, arithmetic and copies ran while one was open for 6% of the time, Pallas kernels for 48%

profile of v2, /device:TPU:0, one launch (start us, length us, event | category | flops | bytes accessed | tf_op | source)
XLA Modules:
  0.0 129.0 jit_solution(10503748249854686878)
XLA Ops:
  0.6 0.5 collective-permute-start.3
  1.2 5.8 %pad_convert_fusion = f32[16392,128]{1,0:T(8,128)} fusion(bf16[16384,128]{1,0:T(8,128)(2,1)} %bitcast.31), kind=kLoop, calls=%fused_computation | loop fusion | flops 2098176 | bytes 12587008 | tf_op jit(solution)/shard_map/jit(_pad)/pad | solution.py:293
  7.0 2.6 %collective-permute-start.4 = (bf16[512,256]{1,0:T(8,128)(2,1)S(1)}, bf16[512,256]{1,0:T(8,128)(2,1)S(1)}, u32[]{:S(2)}, u32[]{:S(2)}) collective-permute-start(bf16[512,256]{1,0:T(8,128)(2,1)S(1)} %pad_maximum_fusion.2), channel_id=1, source_target_pairs={{0,8},{4,12},{8,0},{12,4},{16,24},{20,28},{24,16},{28,20},{1,9},{5... | collective-permute-start | bytes 786440 | tf_op jit(solution)/shard_map/ppermute | solution.py:289
  9.6 0.1 bitcast_select_fusion
  9.7 0.2 reshape.38
  9.9 6.6 %collective-permute-done.4 = bf16[512,256]{1,0:T(8,128)(2,1)S(1)} collective-permute-done((bf16[512,256]{1,0:T(8,128)(2,1)S(1)}, bf16[512,256]{1,0:T(8,128)(2,1)S(1)}, u32[]{:S(2)}, u32[]{:S(2)}) %collective-permute-start.4) | collective-permute-done | bytes 262176 | tf_op jit(solution)/shard_map/ppermute | solution.py:289
  16.5 0.9 pad_maximum_fusion.1
  17.4 1.8 %collective-permute-start.5 = (bf16[1024,256]{1,0:T(8,128)(2,1)}, bf16[1024,256]{1,0:T(8,128)(2,1)}, u32[]{:S(2)}, u32[]{:S(2)}) collective-permute-start(bf16[1024,256]{1,0:T(8,128)(2,1)} %pad_maximum_fusion.1), channel_id=1, source_target_pairs={{0,16},{4,20},{8,24},{12,28},{16,0},{20,4},{24,8},{28,12},{1,17},{... | collective-permute-start | bytes 1572872 | tf_op jit(solution)/shard_map/ppermute | solution.py:289
  19.2 0.2 constant_dynamic-slice_fusion
  19.4 3.4 %copy-done = f32[16392,128]{1,0:T(8,128)S(1)} copy-done((f32[16392,128]{1,0:T(8,128)S(1)}, f32[16392,128]{1,0:T(8,128)}, u32[]{:S(2)}) %copy-start) | copy-done | bytes 8392728
  22.8 15.5 %pool_chunk.4 = bf16[1024,256]{1,0:T(8,128)(2,1)S(1)} custom-call(s32[16384]{0:T(1024)S(1)} %bitcast.27, f32[16392,1,128]{2,1,0:T(1,128)S(1)} %bitcast.19), custom_call_target="tpu_custom_call" | custom-call | flops 209715200 | bytes 16777216 | tf_op jit(solution)/shard_map/pool_chunk/pallas_call | solution.py:41
  38.3 2.7 %collective-permute-start = (bf16[1024,256]{1,0:T(8,128)(2,1)S(1)}, bf16[1024,256]{1,0:T(8,128)(2,1)S(1)}, u32[]{:S(2)}, u32[]{:S(2)}) collective-permute-start(bf16[1024,256]{1,0:T(8,128)(2,1)S(1)} %pool_chunk.4), channel_id=1, source_target_pairs={{0,2},{1,3},{2,0},{3,1},{4,6},{5,7},{6,4},{7,5},{8,10},{9,11},{10,... | collective-permute-start | bytes 1572872 | tf_op jit(solution)/shard_map/ppermute | solution.py:311
  40.9 15.5 %pool_chunk.5 = bf16[1024,256]{1,0:T(8,128)(2,1)S(1)} custom-call(s32[16384]{0:T(1024)S(1)} %bitcast.26, f32[16392,1,128]{2,1,0:T(1,128)S(1)} %bitcast.20), custom_call_target="tpu_custom_call" | custom-call | flops 209715200 | bytes 16777216 | tf_op jit(solution)/shard_map/pool_chunk/pallas_call | solution.py:41
  56.4 1.6 %collective-permute-start.1 = (bf16[1024,256]{1,0:T(8,128)(2,1)S(1)}, bf16[1024,256]{1,0:T(8,128)(2,1)S(1)}, u32[]{:S(2)}, u32[]{:S(2)}) collective-permute-start(bf16[1024,256]{1,0:T(8,128)(2,1)S(1)} %pool_chunk.5), channel_id=1, source_target_pairs={{0,1},{1,2},{2,3},{3,0},{4,5},{5,6},{6,7},{7,4},{8,9},{9,10},{10,1... | collective-permute-start | bytes 1572872 | tf_op jit(solution)/shard_map/ppermute | solution.py:311
  58.1 15.5 %pool_chunk.6 = bf16[1024,256]{1,0:T(8,128)(2,1)S(1)} custom-call(s32[16384]{0:T(1024)S(1)} %bitcast.25, f32[16392,1,128]{2,1,0:T(1,128)S(1)} %bitcast.21), custom_call_target="tpu_custom_call" | custom-call | flops 209715200 | bytes 16777216 | tf_op jit(solution)/shard_map/pool_chunk/pallas_call | solution.py:41
  73.5 2.3 %collective-permute-start.2 = (bf16[1024,256]{1,0:T(8,128)(2,1)S(1)}, bf16[1024,256]{1,0:T(8,128)(2,1)S(1)}, u32[]{:S(2)}, u32[]{:S(2)}) collective-permute-start(bf16[1024,256]{1,0:T(8,128)(2,1)S(1)} %pool_chunk.6), channel_id=1, source_target_pairs={{0,3},{1,0},{2,1},{3,2},{4,7},{5,4},{6,5},{7,6},{8,11},{9,8},{10,9... | collective-permute-start | bytes 1572872 | tf_op jit(solution)/shard_map/ppermute | solution.py:311
  75.8 3.4 %copy-done.2 = f32[16392,128]{1,0:T(8,128)S(1)} copy-done((f32[16392,128]{1,0:T(8,128)S(1)}, f32[16392,128]{1,0:T(8,128)}, u32[]{:S(2)}) %copy-start.2) | copy-done | bytes 8392728
  79.2 15.5 %pool_chunk.7.refs_3_ = bf16[1024,256]{1,0:T(8,128)(2,1)S(1)} custom-call(s32[16384]{0:T(1024)S(1)} %bitcast.24, f32[16392,1,128]{2,1,0:T(1,128)S(1)} %bitcast.22), custom_call_target="tpu_custom_call" | custom-call | flops 209715200 | bytes 16777216 | tf_op jit(solution)/shard_map/pool_chunk/pallas_call | solution.py:41
  94.7 0.0 copy-start.4
  94.8 0.1 pad_add_fusion.me_ref
  94.8 1.2 pad_maximum_fusion.refs_8_
  96.1 16.2 %tower_and_softmax.1 = (f32[1,1024]{1,0:T(1,128)}, f32[1024,256]{1,0:T(8,128)}, bf16[2048,256]{1,0:T(8,128)(2,1)S(1)}) custom-call(s32[2]{0:T(128)S(1)} %pad_add_fusion.me_ref, s32[2,16]{1,0:T(2,128)S(1)} %copy-done.6, bf16[1024,256]{1,0:T(8,128)(2,1)S(1)} %collective-permute-done.refs_0_, bf16[1024,256]{1,0:T(8,128)(2,1)S(1)} %collective-permute-done.1.refs_1_, ...), custom_call_target="tpu_custom_call" | custom-call | tf_op jit(solution)/shard_map/tower_and_softmax/pallas_call | solution.py:150
  112.3 16.1 %reduce_item_grad.1 = f32[64,256]{1,0:T(8,128)S(1)} custom-call(bf16[4,2,256,256]{3,2,1,0:T(8,128)(2,1)S(1)} %bitcast.23), custom_call_target="tpu_custom_call" | custom-call | tf_op jit(solution)/shard_map/reduce_item_grad/pallas_call | solution.py:253
  128.4 0.6 copy.14
  (30 shorter events, 0.1 us)
Async XLA Ops:
  0.6 6.3 %collective-permute-start.3 = (bf16[256,256]{1,0:T(8,128)(2,1)}, bf16[256,256]{1,0:T(8,128)(2,1)S(1)}, u32[]{:S(2)}, u32[]{:S(2)}) collective-permute-start(bf16[256,256]{1,0:T(8,128)(2,1)} %param.17), channel_id=1, source_target_pairs={{0,4},{4,0},{8,12},{12,8},{16,20},{20,16},{24,28},{28,24},{1,5},{5... | collective-permute-start | bytes 393224 | tf_op jit(solution)/shard_map/ppermute | solution.py:289
  1.1 5.8 %copy-start.8 = (bf16[256,256]{1,0:T(8,128)(2,1)S(1)}, bf16[256,256]{1,0:T(8,128)(2,1)}, u32[]{:S(2)}) copy-start(bf16[256,256]{1,0:T(8,128)(2,1)} %param.17) | copy-start | bytes 393220
  1.2 8.4 %copy-start.11 = (s32[4096,2,8]{0,2,1:T(8,128)S(1)}, s32[4096,2,8]{0,2,1:T(8,128)}, u32[]{:S(2)}) copy-start(s32[4096,2,8]{0,2,1:T(8,128)} %param.11) | copy-start | bytes 786436
  1.2 8.4 %copy-start.12 = (s32[4096,2]{0,1:T(2,128)S(1)}, s32[4096,2]{0,1:T(2,128)}, u32[]{:S(2)}) copy-start(s32[4096,2]{0,1:T(2,128)} %param.12) | copy-start | bytes 98308
  7.0 9.5 %collective-permute-start.4 = (bf16[512,256]{1,0:T(8,128)(2,1)S(1)}, bf16[512,256]{1,0:T(8,128)(2,1)S(1)}, u32[]{:S(2)}, u32[]{:S(2)}) collective-permute-start(bf16[512,256]{1,0:T(8,128)(2,1)S(1)} %pad_maximum_fusion.2), channel_id=1, source_target_pairs={{0,8},{4,12},{8,0},{12,4},{16,24},{20,28},{24,16},{28,20},{1,9},{5... | collective-permute-start | bytes 786440 | tf_op jit(solution)/shard_map/ppermute | solution.py:289
  16.5 21.7 %copy-start.9 = (bf16[512,256]{1,0:T(8,128)(2,1)}, bf16[512,256]{1,0:T(8,128)(2,1)S(1)}, u32[]{:S(2)}) copy-start(bf16[512,256]{1,0:T(8,128)(2,1)S(1)} %collective-permute-done.4) | copy-start | bytes 786436
  17.4 77.4 %collective-permute-start.5 = (bf16[1024,256]{1,0:T(8,128)(2,1)}, bf16[1024,256]{1,0:T(8,128)(2,1)}, u32[]{:S(2)}, u32[]{:S(2)}) collective-permute-start(bf16[1024,256]{1,0:T(8,128)(2,1)} %pad_maximum_fusion.1), channel_id=1, source_target_pairs={{0,16},{4,20},{8,24},{12,28},{16,0},{20,4},{24,8},{28,12},{1,17},{... | collective-permute-start | bytes 1572872 | tf_op jit(solution)/shard_map/ppermute | solution.py:289
  19.4 3.4 %copy-start = (f32[16392,128]{1,0:T(8,128)S(1)}, f32[16392,128]{1,0:T(8,128)}, u32[]{:S(2)}) copy-start(f32[16392,128]{1,0:T(8,128)} %pad_convert_fusion) | copy-start | bytes 25178116
  22.8 18.1 %copy-start.1 = (f32[16392,128]{1,0:T(8,128)S(1)}, f32[16392,128]{1,0:T(8,128)}, u32[]{:S(2)}) copy-start(f32[16392,128]{1,0:T(8,128)} %pad_convert_fusion) | copy-start | bytes 25178116
  38.3 57.8 %collective-permute-start = (bf16[1024,256]{1,0:T(8,128)(2,1)S(1)}, bf16[1024,256]{1,0:T(8,128)(2,1)S(1)}, u32[]{:S(2)}, u32[]{:S(2)}) collective-permute-start(bf16[1024,256]{1,0:T(8,128)(2,1)S(1)} %pool_chunk.4), channel_id=1, source_target_pairs={{0,2},{1,3},{2,0},{3,1},{4,6},{5,7},{6,4},{7,5},{8,10},{9,11},{10,... | collective-permute-start | bytes 1572872 | tf_op jit(solution)/shard_map/ppermute | solution.py:311
  56.4 39.6 %collective-permute-start.1 = (bf16[1024,256]{1,0:T(8,128)(2,1)S(1)}, bf16[1024,256]{1,0:T(8,128)(2,1)S(1)}, u32[]{:S(2)}, u32[]{:S(2)}) collective-permute-start(bf16[1024,256]{1,0:T(8,128)(2,1)S(1)} %pool_chunk.5), channel_id=1, source_target_pairs={{0,1},{1,2},{2,3},{3,0},{4,5},{5,6},{6,7},{7,4},{8,9},{9,10},{10,1... | collective-permute-start | bytes 1572872 | tf_op jit(solution)/shard_map/ppermute | solution.py:311
  73.5 22.5 %collective-permute-start.2 = (bf16[1024,256]{1,0:T(8,128)(2,1)S(1)}, bf16[1024,256]{1,0:T(8,128)(2,1)S(1)}, u32[]{:S(2)}, u32[]{:S(2)}) collective-permute-start(bf16[1024,256]{1,0:T(8,128)(2,1)S(1)} %pool_chunk.6), channel_id=1, source_target_pairs={{0,3},{1,0},{2,1},{3,2},{4,7},{5,4},{6,5},{7,6},{8,11},{9,8},{10,9... | collective-permute-start | bytes 1572872 | tf_op jit(solution)/shard_map/ppermute | solution.py:311
  75.8 3.4 %copy-start.2 = (f32[16392,128]{1,0:T(8,128)S(1)}, f32[16392,128]{1,0:T(8,128)}, u32[]{:S(2)}) copy-start(f32[16392,128]{1,0:T(8,128)} %pad_convert_fusion) | copy-start | bytes 25178116
  79.2 15.6 %copy-start.10 = (bf16[512,256]{1,0:T(8,128)(2,1)S(1)}, bf16[512,256]{1,0:T(8,128)(2,1)}, u32[]{:S(2)}) copy-start(bf16[512,256]{1,0:T(8,128)(2,1)} %copy-done.9) | copy-start | bytes 786436
  94.7 1.4 %copy-start.3 = (bf16[1024,256]{1,0:T(8,128)(2,1)S(1)}, bf16[1024,256]{1,0:T(8,128)(2,1)}, u32[]{:S(2)}) copy-start(bf16[1024,256]{1,0:T(8,128)(2,1)} %refs_6_.1) | copy-start | bytes 1572868
  94.7 1.4 %copy-start.4 = (f32[1024]{0:T(1024)S(1)}, f32[1024]{0:T(1024)}, u32[]{:S(2)}) copy-start(f32[1024]{0:T(1024)} %param.14) | copy-start | bytes 12292
  94.7 1.4 %copy-start.5 = (s32[1024]{0:T(1024)S(1)}, s32[1024]{0:T(1024)}, u32[]{:S(2)}) copy-start(s32[1024]{0:T(1024)} %param.19) | copy-start | bytes 12292
  94.7 1.4 %copy-start.6 = (s32[2,16]{1,0:T(2,128)S(1)}, s32[2,16]{1,0:T(2,128)}, u32[]{:S(2)}) copy-start(s32[2,16]{1,0:T(2,128)} %elig_ref.1) | copy-start | bytes 388
  94.7 1.4 %copy-start.7 = (f32[256]{0:T(256)S(1)}, f32[256]{0:T(256)}, u32[]{:S(2)}) copy-start(f32[256]{0:T(256)} %param.16) | copy-start | bytes 3076

commit v3 on v2

--- a/solution.py
+++ b/solution.py
@@ -8,6 +8,7 @@
 from jax.sharding import PartitionSpec as P
 
 masked_value = -1e30
+UNROLL = 32
 MIB = 1 << 20
 MESH = pl.DeviceIdType.MESH
 
@@ -17,8 +18,8 @@
     width = table_ref.shape[2]
 
     def group(step, carry):
-        first = pl.multiple_of(step * 8, 8)
-        for user in range(8):
+        first = pl.multiple_of(step * UNROLL, UNROLL)
+        for user in range(UNROLL):
             for feature in range(features):
                 rows = [
                     table_ref[ids_ref[first + ((feature * bag + entry) * users + user)]]
@@ -32,7 +33,7 @@
                 sums_ref[step, user : user + 1, feature * width : (feature + 1) * width] = rows[0]
         return carry
 
-    lax.fori_loop(0, users // 8, group, 0)
+    lax.fori_loop(0, users // UNROLL, group, 0)
     out_ref[...] = sums_ref[...].reshape(out_ref.shape).astype(out_ref.dtype)
 
 
@@ -46,8 +47,8 @@
             pl.BlockSpec(memory_space=pltpu.VMEM),
         ],
         out_specs=pl.BlockSpec(memory_space=pltpu.VMEM),
-        scratch_shapes=[pltpu.VMEM((users // 8, 8, features * width), jnp.float32)],
-        compiler_params=pltpu.CompilerParams(vmem_limit_bytes=20 * MIB),
+        scratch_shapes=[pltpu.VMEM((users // UNROLL, UNROLL, features * width), jnp.float32)],
+        compiler_params=pltpu.CompilerParams(vmem_limit_bytes=12 * MIB),
         cost_estimate=pl.CostEstimate(
             flops=users * features * bag * width * 100, bytes_accessed=16 * MIB, transcendentals=0
         ),
@@ -136,7 +137,9 @@
 
     @pl.when(tile == pl.num_programs(0) - 1)
     def _():
-        igrad_ref[...] = acc_ref[...].astype(igrad_ref.dtype)
+        half = igrad_ref.shape[2]
+        for h in range(igrad_ref.shape[0]):
+            igrad_ref[h] = acc_ref[:, h * half : (h + 1) * half].astype(igrad_ref.dtype)
 
 
 def main_call(order, owned, me, pieces, w_hidden, b_hidden, w_out, b_out, items, elig, positives):
@@ -153,7 +156,7 @@
         out_shape=(
             jax.ShapeDtypeStruct((1, users), jnp.float32),
             jax.ShapeDtypeStruct((users, width), jnp.float32),
-            jax.ShapeDtypeStruct((count, width), jnp.bfloat16),
+            jax.ShapeDtypeStruct((2, count, width // 2), jnp.bfloat16),
         ),
         in_specs=[smem, smem]
         + [pl.BlockSpec((tile_users, depth), lambda i: (i, 0))] * len(order)
@@ -168,7 +171,7 @@
         out_specs=(
             pl.BlockSpec((1, tile_users), lambda i: (0, i)),
             pl.BlockSpec((tile_users, width), lambda i: (i, 0)),
-            whole((count, width)),
+            pl.BlockSpec((2, count, width // 2), lambda i: (0, 0, 0)),
         ),
         scratch_shapes=[
             pltpu.VMEM((count, width), jnp.bfloat16),
@@ -205,65 +208,73 @@
         pl.semaphore_signal(barrier, inc=1, device_id=partner, device_id_type=MESH)
     pl.semaphore_wait(barrier, len(partners))
 
-    copy = pltpu.make_async_remote_copy(
-        src_ref=part_ref.at[:, 1 - core], dst_ref=got_a, send_sem=send_a, recv_sem=recv_a,
-        device_id=other_core, device_id_type=MESH,
-    )
-    copy.start()
-    copy.wait()
-    sum_a[...] = (
-        part_ref[:, core].astype(jnp.float32) + got_a[...].astype(jnp.float32)
-    ).astype(sum_a.dtype)
-
-    copies = []
-    for k in range(1, chips):
-        copies.append(pltpu.make_async_remote_copy(
-            src_ref=sum_a.at[lax.rem(chip + k, chips)], dst_ref=got_b.at[k - 1],
-            send_sem=send_b.at[k - 1], recv_sem=recv_b.at[k - 1],
-            device_id=chip_at(k), device_id_type=MESH,
+    rows = out_ref.shape[0]
+    halves = part_ref.shape[0]
+    half = part_ref.shape[4]
+    first = []
+    for h in range(halves):
+        first.append(pltpu.make_async_remote_copy(
+            src_ref=part_ref.at[h, :, 1 - core], dst_ref=got_a.at[h],
+            send_sem=send_a.at[h], recv_sem=recv_a.at[h],
+            device_id=other_core, device_id_type=MESH,
         ))
-        copies[-1].start()
-    total = sum_a[chip].astype(jnp.float32)
-    for k in range(1, chips):
-        copies[k - 1].wait()
-        total += got_b[k - 1].astype(jnp.float32)
-    rows = out_ref.shape[0]
-    sum_b[...] = total.astype(sum_b.dtype).reshape(shards, rows, total.shape[1])
-
-    copies = []
-    for k in range(1, shards):
-        copies.append(pltpu.make_async_remote_copy(
-            src_ref=sum_b.at[lax.rem(shard + k, shards)], dst_ref=got_c.at[k - 1],
-            send_sem=send_c.at[k - 1], recv_sem=recv_c.at[k - 1],
-            device_id=shard_at(k), device_id_type=MESH,
-        ))
-        copies[-1].start()
-    total = sum_b[shard].astype(jnp.float32)
-    for k in range(1, shards):
-        copies[k - 1].wait()
-        total += got_c[k - 1].astype(jnp.float32)
-    out_ref[...] = total
+        first[h].start()
+    second = []
+    for h in range(halves):
+        first[h].wait()
+        sum_a[h] = (
+            part_ref[h, :, core].astype(jnp.float32) + got_a[h].astype(jnp.float32)
+        ).astype(sum_a.dtype)
+        second.append([])
+        for k in range(1, chips):
+            second[h].append(pltpu.make_async_remote_copy(
+                src_ref=sum_a.at[h, lax.rem(chip + k, chips)], dst_ref=got_b.at[h, k - 1],
+                send_sem=send_b.at[h, k - 1], recv_sem=recv_b.at[h, k - 1],
+                device_id=chip_at(k), device_id_type=MESH,
+            ))
+            second[h][-1].start()
+    third = []
+    for h in range(halves):
+        total = sum_a[h, chip].astype(jnp.float32)
+        for k in range(1, chips):
+            second[h][k - 1].wait()
+            total += got_b[h, k - 1].astype(jnp.float32)
+        sum_b[h] = total.astype(sum_b.dtype).reshape(shards, rows, half)
+        third.append([])
+        for k in range(1, shards):
+            third[h].append(pltpu.make_async_remote_copy(
+                src_ref=sum_b.at[h, lax.rem(shard + k, shards)], dst_ref=got_c.at[h, k - 1],
+                send_sem=send_c.at[h, k - 1], recv_sem=recv_c.at[h, k - 1],
+                device_id=shard_at(k), device_id_type=MESH,
+            ))
+            third[h][-1].start()
+    for h in range(halves):
+        total = sum_b[h, shard].astype(jnp.float32)
+        for k in range(1, shards):
+            third[h][k - 1].wait()
+            total += got_c[h, k - 1].astype(jnp.float32)
+        out_ref[:, h * half : (h + 1) * half] = total
 
 
 def reduce_call(partial):
-    chips, _, rows, width = partial.shape
+    halves, chips, _, rows, half = partial.shape
     shards = lax.axis_size("tbl")
     piece = rows // shards
     dma = pltpu.SemaphoreType.DMA
     return pl.pallas_call(
         functools.partial(reduce_kernel, chips, shards),
-        out_shape=jax.ShapeDtypeStruct((piece, width), jnp.float32),
+        out_shape=jax.ShapeDtypeStruct((piece, halves * half), jnp.float32),
         in_specs=[pl.BlockSpec(memory_space=pltpu.VMEM)],
         out_specs=pl.BlockSpec(memory_space=pltpu.VMEM),
         scratch_shapes=[
-            pltpu.VMEM((chips, rows, width), jnp.bfloat16),
-            pltpu.VMEM((chips, rows, width), jnp.bfloat16),
-            pltpu.VMEM((chips - 1, rows, width), jnp.bfloat16),
-            pltpu.VMEM((shards, piece, width), jnp.bfloat16),
-            pltpu.VMEM((shards - 1, piece, width), jnp.bfloat16),
-            dma, dma,
-            dma((chips - 1,)), dma((chips - 1,)),
-            dma((shards - 1,)), dma((shards - 1,)),
+            pltpu.VMEM((halves, chips, rows, half), jnp.bfloat16),
+            pltpu.VMEM((halves, chips, rows, half), jnp.bfloat16),
+            pltpu.VMEM((halves, chips - 1, rows, half), jnp.bfloat16),
+            pltpu.VMEM((halves, shards, piece, half), jnp.bfloat16),
+            pltpu.VMEM((halves, shards - 1, piece, half), jnp.bfloat16),
+            dma((halves,)), dma((halves,)),
+            dma((halves, chips - 1)), dma((halves, chips - 1)),
+            dma((halves, shards - 1)), dma((halves, shards - 1)),
         ],
         compiler_params=pltpu.CompilerParams(
             collective_id=0, has_side_effects=True, vmem_limit_bytes=24 * MIB
@@ -280,14 +291,6 @@
     group_users, features, bag = feat_ids.shape
     users = group_users // shards
     rows, width = tables.shape[1:]
-
-    cycle = lax.axis_size("item")
-    items = item_vecs
-    reach = 1
-    while reach < cycle:
-        pairs = [(source, source ^ reach) for source in range(cycle)]
-        items = jnp.concatenate([items, lax.ppermute(items, "item", pairs)])
-        reach *= 2
 
     zero_row = features * rows
     table = jnp.pad(tables.reshape(zero_row, width).astype(jnp.float32), ((0, 8), (0, 0)))
@@ -300,23 +303,35 @@
     ids = jnp.transpose(ids.reshape(features * bag, shards, users), (1, 0, 2))
     ids = ids.reshape(shards, features * bag * users)
 
+    cycle = lax.axis_size("item")
+    items = item_vecs
+    reach = 1
     order = sorted(range(1, shards), key=lambda d: (abs(2 * d - shards), d)) + [0]
     pieces = []
     for distance in order:
         target = lax.rem(me + distance, shards)
         chunk = lax.dynamic_index_in_dim(ids, target, 0, keepdims=False)
+        arrived = None
+        if reach < cycle:
+            pairs = [(source, source ^ reach) for source in range(cycle)]
+            arrived = lax.ppermute(items, "item", pairs)
+            reach *= 2
         pooled = pool_chunk(chunk, table, users, features, bag)
+        if arrived is not None:
+            arrived, pooled = lax.optimization_barrier((arrived, pooled))
+            items = jnp.concatenate([items, arrived])
         if distance:
             pairs = [(source, (source + distance) % shards) for source in range(shards)]
             pooled = lax.ppermute(pooled, "tbl", pairs)
         pieces.append(pooled)
+    assert reach == cycle
 
     loss, user_grad, partial = main_call(
         tuple(order), item_vecs.shape[0],
         jnp.stack([me, lax.axis_index("item")]).astype(jnp.int32), pieces, w_hidden, b_hidden, w_out, b_out,
         items, elig_mask, positives,
     )
-    partial = partial.reshape(cycle // 2, 2, item_vecs.shape[0], item_vecs.shape[1])
+    partial = partial.reshape(2, cycle // 2, 2, item_vecs.shape[0], item_vecs.shape[1] // 2)
     item_grad = reduce_call(partial)
     return (loss.reshape(users), user_grad, item_grad)
 

time: 129 us -> 141 us (1.093)
  waiting for transfers between devices: 6.62 us -> 13.9 us
  Pallas kernels: 94.2 us -> 99.3 us
    ppermute x3, waiting for transfers between devices: 0.01 us -> 13.8 us  [local(): pooled = lax.ppermute(pooled, 'tbl', pairs)]
    pallas_call x1, Pallas kernels: 16.1 us -> 23.8 us  [reduce_call(): pl.pallas_call(functools.partial(reduce_kernel, chips, shards), out_shape...]
    ppermute x3, waiting for transfers between devices: 6.61 us -> 0.01 us  [local(): arrived = lax.ppermute(items, 'item', pairs)]
    pallas_call x4, Pallas kernels: 61.9 us -> 59.3 us  [pool_chunk(): pl.pallas_call(functools.partial(pool_kernel, features, bag), out_shape=j...]
    concatenate x3, other arithmetic: 2.08 us -> 0.12 us  [local(): items = jnp.concatenate([items, arrived])]
  transfers between devices with their start and end apart: 6 -> 6, of which waited for: 1 -> 2; matrix products, arithmetic and copies ran while one was open for 6% -> 5% of each run, Pallas kernels for 48% -> 42%
where the time goes in v3:
time: 141 us
  Pallas kernels  99.3 us (70%)
  waiting for transfers between devices  13.9 us (10%)
  starting transfers between devices  11.2 us (8%)
  local copies, waits for them, and re-layouts  8.64 us (6%)
  other arithmetic  7.01 us (5%)
    pallas_call x4, Pallas kernels, pool_chunk(): pl.pallas_call(functools.partial(pool_kernel, features, bag), out_shape=j...  59.3 us
    pallas_call x1, Pallas kernels, reduce_call(): pl.pallas_call(functools.partial(reduce_kernel, chips, shards), out_shape...  23.8 us
    pallas_call x1, Pallas kernels, main_call(): pl.pallas_call(functools.partial(main_kernel, order, owned), grid=(tiles,...  16.2 us
    ppermute x3, waiting for transfers between devices, local(): pooled = lax.ppermute(pooled, 'tbl', pairs)  13.8 us
    unnamed x27, local copies, waits for them, and re-layouts  8.23 us
    ppermute x3, starting transfers between devices, local(): pooled = lax.ppermute(pooled, 'tbl', pairs)  6.48 us
    pad x1, other arithmetic, local(): jnp.pad(tables.reshape(zero_row, width).astype(jnp.float32), ((0, 8), (0,...  5.76 us
    ppermute x3, starting transfers between devices, local(): arrived = lax.ppermute(items, 'item', pairs)  4.7 us
  transfers between devices with their start and end apart: 6, of which 2 were waited for; matrix products, arithmetic and copies ran while one was open for 5% of the time, Pallas kernels for 42%

profile of v3, /device:TPU:0, one launch (start us, length us, event | category | flops | bytes accessed | tf_op | source)
XLA Modules:
  0.0 140.8 jit_solution(9311760446700376080)
XLA Ops:
  0.6 0.5 collective-permute-start
  1.2 1.0 bitcast_select_fusion
  2.2 0.2 reshape.38
  2.4 5.8 %pad_convert_fusion = f32[16392,128]{1,0:T(8,128)} fusion(bf16[16384,128]{1,0:T(8,128)(2,1)} %bitcast.31), kind=kLoop, calls=%fused_computation | loop fusion | flops 2098176 | bytes 12587008 | tf_op jit(solution)/shard_map/jit(_pad)/pad | solution.py:296
  8.1 0.2 constant_dynamic-slice_fusion
  8.4 3.4 %copy-done = f32[16392,128]{1,0:T(8,128)S(1)} copy-done((f32[16392,128]{1,0:T(8,128)S(1)}, f32[16392,128]{1,0:T(8,128)}, u32[]{:S(2)}) %copy-start) | copy-done | bytes 8392728
  11.8 14.8 %pool_chunk.4 = bf16[1024,256]{1,0:T(8,128)(2,1)S(1)} custom-call(s32[16384]{0:T(1024)S(1)} %bitcast.27, f32[16392,1,128]{2,1,0:T(1,128)S(1)} %bitcast.19), custom_call_target="tpu_custom_call" | custom-call | flops 209715200 | bytes 16777216 | tf_op jit(solution)/shard_map/pool_chunk/pallas_call | solution.py:42
  26.6 2.6 %collective-permute-start.2 = (bf16[512,256]{1,0:T(8,128)(2,1)S(1)}, bf16[512,256]{1,0:T(8,128)(2,1)S(1)}, u32[]{:S(2)}, u32[]{:S(2)}) collective-permute-start(bf16[512,256]{1,0:T(8,128)(2,1)S(1)} %pad_maximum_fusion.2), channel_id=1, source_target_pairs={{0,8},{4,12},{8,0},{12,4},{16,24},{20,28},{24,16},{28,20},{1,9},{5... | collective-permute-start | bytes 786440 | tf_op jit(solution)/shard_map/ppermute | solution.py:317
  29.2 14.8 %pool_chunk.5 = bf16[1024,256]{1,0:T(8,128)(2,1)S(1)} custom-call(s32[16384]{0:T(1024)S(1)} %bitcast.26, f32[16392,1,128]{2,1,0:T(1,128)S(1)} %bitcast.20), custom_call_target="tpu_custom_call" | custom-call | flops 209715200 | bytes 16777216 | tf_op jit(solution)/shard_map/pool_chunk/pallas_call | solution.py:42
  44.1 1.6 %collective-permute-start.4 = (bf16[1024,256]{1,0:T(8,128)(2,1)S(1)}, bf16[1024,256]{1,0:T(8,128)(2,1)S(1)}, u32[]{:S(2)}, u32[]{:S(2)}) collective-permute-start(bf16[1024,256]{1,0:T(8,128)(2,1)S(1)} %pad_maximum_fusion.1), channel_id=1, source_target_pairs={{0,16},{4,20},{8,24},{12,28},{16,0},{20,4},{24,8},{28,12},{1,17},{... | collective-permute-start | bytes 1572872 | tf_op jit(solution)/shard_map/ppermute | solution.py:317
  45.7 14.8 %pool_chunk.6 = bf16[1024,256]{1,0:T(8,128)(2,1)S(1)} custom-call(s32[16384]{0:T(1024)S(1)} %bitcast.25, f32[16392,1,128]{2,1,0:T(1,128)S(1)} %bitcast.21), custom_call_target="tpu_custom_call" | custom-call | flops 209715200 | bytes 16777216 | tf_op jit(solution)/shard_map/pool_chunk/pallas_call | solution.py:42
  60.5 2.7 %collective-permute-start.1 = (bf16[1024,256]{1,0:T(8,128)(2,1)S(1)}, bf16[1024,256]{1,0:T(8,128)(2,1)S(1)}, u32[]{:S(2)}, u32[]{:S(2)}) collective-permute-start(bf16[1024,256]{1,0:T(8,128)(2,1)S(1)} %pool_chunk.4), channel_id=1, source_target_pairs={{0,2},{1,3},{2,0},{3,1},{4,6},{5,7},{6,4},{7,5},{8,10},{9,11},{10,... | collective-permute-start | bytes 1572872 | tf_op jit(solution)/shard_map/ppermute | solution.py:325
  63.2 1.6 %collective-permute-start.3 = (bf16[1024,256]{1,0:T(8,128)(2,1)S(1)}, bf16[1024,256]{1,0:T(8,128)(2,1)S(1)}, u32[]{:S(2)}, u32[]{:S(2)}) collective-permute-start(bf16[1024,256]{1,0:T(8,128)(2,1)S(1)} %pool_chunk.5), channel_id=1, source_target_pairs={{0,1},{1,2},{2,3},{3,0},{4,5},{5,6},{6,7},{7,4},{8,9},{9,10},{10,1... | collective-permute-start | bytes 1572872 | tf_op jit(solution)/shard_map/ppermute | solution.py:325
  64.8 0.8 copy-done.11
  65.6 2.2 %collective-permute-start.5 = (bf16[1024,256]{1,0:T(8,128)(2,1)S(1)}, bf16[1024,256]{1,0:T(8,128)(2,1)S(1)}, u32[]{:S(2)}, u32[]{:S(2)}) collective-permute-start(bf16[1024,256]{1,0:T(8,128)(2,1)S(1)} %pool_chunk.6), channel_id=1, source_target_pairs={{0,3},{1,0},{2,1},{3,2},{4,7},{5,4},{6,5},{7,6},{8,11},{9,8},{10,9... | collective-permute-start | bytes 1572872 | tf_op jit(solution)/shard_map/ppermute | solution.py:325
  67.8 3.4 %copy-done.2 = f32[16392,128]{1,0:T(8,128)S(1)} copy-done((f32[16392,128]{1,0:T(8,128)S(1)}, f32[16392,128]{1,0:T(8,128)}, u32[]{:S(2)}) %copy-start.2) | copy-done | bytes 8392728
  71.2 14.8 %pool_chunk.7.refs_3_ = bf16[1024,256]{1,0:T(8,128)(2,1)S(1)} custom-call(s32[16384]{0:T(1024)S(1)} %bitcast.24, f32[16392,1,128]{2,1,0:T(1,128)S(1)} %bitcast.22), custom_call_target="tpu_custom_call" | custom-call | flops 209715200 | bytes 16777216 | tf_op jit(solution)/shard_map/pool_chunk/pallas_call | solution.py:42
  86.1 0.1 pad_add_fusion.me_ref
  86.2 0.1 pad_maximum_fusion.refs_8_
  86.2 12.6 %collective-permute-done.1.refs_0_ = bf16[1024,256]{1,0:T(8,128)(2,1)S(1)} collective-permute-done((bf16[1024,256]{1,0:T(8,128)(2,1)S(1)}, bf16[1024,256]{1,0:T(8,128)(2,1)S(1)}, u32[]{:S(2)}, u32[]{:S(2)}) %collective-permute-start.1) | collective-permute-done | bytes 524320 | tf_op jit(solution)/shard_map/ppermute | solution.py:325
  98.8 1.3 collective-permute-done.5.refs_2_
  100.1 16.2 %tower_and_softmax.1 = (f32[1,1024]{1,0:T(1,128)}, f32[1024,256]{1,0:T(8,128)}, bf16[2,2048,128]{2,1,0:T(8,128)(2,1)S(1)}) custom-call(s32[2]{0:T(128)S(1)} %pad_add_fusion.me_ref, s32[2,16]{1,0:T(2,128)S(1)} %copy-done.6, bf16[1024,256]{1,0:T(8,128)(2,1)S(1)} %collective-permute-done.1.refs_0_, bf16[1024,256]{1,0:T(8,128)(2,1)S(1)} %collective-permute-done.3.refs_1_, ...), custom_call_target="tpu_custom_call" | custom-call | tf_op jit(solution)/shard_map/tower_and_softmax/pallas_call | solution.py:153
  116.3 23.8 %reduce_item_grad.1 = f32[64,256]{1,0:T(8,128)S(1)} custom-call(bf16[2,4,2,256,128]{4,3,2,1,0:T(8,128)(2,1)S(1)} %bitcast.23), custom_call_target="tpu_custom_call" | custom-call | tf_op jit(solution)/shard_map/reduce_item_grad/pallas_call | solution.py:264
  140.2 0.6 copy.14
  (30 shorter events, 0.1 us)
Async XLA Ops:
  0.6 26.0 %collective-permute-start = (bf16[256,256]{1,0:T(8,128)(2,1)}, bf16[256,256]{1,0:T(8,128)(2,1)S(1)}, u32[]{:S(2)}, u32[]{:S(2)}) collective-permute-start(bf16[256,256]{1,0:T(8,128)(2,1)} %param.17), channel_id=1, source_target_pairs={{0,4},{4,0},{8,12},{12,8},{16,20},{20,16},{24,28},{28,24},{1,5},{5... | collective-permute-start | bytes 393224 | tf_op jit(solution)/shard_map/ppermute | solution.py:317
  8.4 3.4 %copy-start = (f32[16392,128]{1,0:T(8,128)S(1)}, f32[16392,128]{1,0:T(8,128)}, u32[]{:S(2)}) copy-start(f32[16392,128]{1,0:T(8,128)} %pad_convert_fusion) | copy-start | bytes 25178116
  11.8 14.8 %copy-start.8 = (bf16[256,256]{1,0:T(8,128)(2,1)S(1)}, bf16[256,256]{1,0:T(8,128)(2,1)}, u32[]{:S(2)}) copy-start(bf16[256,256]{1,0:T(8,128)(2,1)} %param.17) | copy-start | bytes 393220
  11.8 17.5 %copy-start.1 = (f32[16392,128]{1,0:T(8,128)S(1)}, f32[16392,128]{1,0:T(8,128)}, u32[]{:S(2)}) copy-start(f32[16392,128]{1,0:T(8,128)} %pad_convert_fusion) | copy-start | bytes 25178116
  26.6 17.4 %collective-permute-start.2 = (bf16[512,256]{1,0:T(8,128)(2,1)S(1)}, bf16[512,256]{1,0:T(8,128)(2,1)S(1)}, u32[]{:S(2)}, u32[]{:S(2)}) collective-permute-start(bf16[512,256]{1,0:T(8,128)(2,1)S(1)} %pad_maximum_fusion.2), channel_id=1, source_target_pairs={{0,8},{4,12},{8,0},{12,4},{16,24},{20,28},{24,16},{28,20},{1,9},{5... | collective-permute-start | bytes 786440 | tf_op jit(solution)/shard_map/ppermute | solution.py:317
  44.1 16.5 %copy-start.9 = (bf16[512,256]{1,0:T(8,128)(2,1)}, bf16[512,256]{1,0:T(8,128)(2,1)S(1)}, u32[]{:S(2)}) copy-start(bf16[512,256]{1,0:T(8,128)(2,1)S(1)} %collective-permute-done.2) | copy-start | bytes 786436
  44.1 20.7 %collective-permute-start.4 = (bf16[1024,256]{1,0:T(8,128)(2,1)S(1)}, bf16[1024,256]{1,0:T(8,128)(2,1)S(1)}, u32[]{:S(2)}, u32[]{:S(2)}) collective-permute-start(bf16[1024,256]{1,0:T(8,128)(2,1)S(1)} %pad_maximum_fusion.1), channel_id=1, source_target_pairs={{0,16},{4,20},{8,24},{12,28},{16,0},{20,4},{24,8},{28,12},{1,17},{... | collective-permute-start | bytes 1572872 | tf_op jit(solution)/shard_map/ppermute | solution.py:317
  60.5 38.3 %collective-permute-start.1 = (bf16[1024,256]{1,0:T(8,128)(2,1)S(1)}, bf16[1024,256]{1,0:T(8,128)(2,1)S(1)}, u32[]{:S(2)}, u32[]{:S(2)}) collective-permute-start(bf16[1024,256]{1,0:T(8,128)(2,1)S(1)} %pool_chunk.4), channel_id=1, source_target_pairs={{0,2},{1,3},{2,0},{3,1},{4,6},{5,7},{6,4},{7,5},{8,10},{9,11},{10,... | collective-permute-start | bytes 1572872 | tf_op jit(solution)/shard_map/ppermute | solution.py:325
  63.2 35.6 %collective-permute-start.3 = (bf16[1024,256]{1,0:T(8,128)(2,1)S(1)}, bf16[1024,256]{1,0:T(8,128)(2,1)S(1)}, u32[]{:S(2)}, u32[]{:S(2)}) collective-permute-start(bf16[1024,256]{1,0:T(8,128)(2,1)S(1)} %pool_chunk.5), channel_id=1, source_target_pairs={{0,1},{1,2},{2,3},{3,0},{4,5},{5,6},{6,7},{7,4},{8,9},{9,10},{10,1... | collective-permute-start | bytes 1572872 | tf_op jit(solution)/shard_map/ppermute | solution.py:325
  64.8 0.8 copy-start.11
  65.6 34.5 %collective-permute-start.5 = (bf16[1024,256]{1,0:T(8,128)(2,1)S(1)}, bf16[1024,256]{1,0:T(8,128)(2,1)S(1)}, u32[]{:S(2)}, u32[]{:S(2)}) collective-permute-start(bf16[1024,256]{1,0:T(8,128)(2,1)S(1)} %pool_chunk.6), channel_id=1, source_target_pairs={{0,3},{1,0},{2,1},{3,2},{4,7},{5,4},{6,5},{7,6},{8,11},{9,8},{10,9... | collective-permute-start | bytes 1572872 | tf_op jit(solution)/shard_map/ppermute | solution.py:325
  67.8 3.4 %copy-start.2 = (f32[16392,128]{1,0:T(8,128)S(1)}, f32[16392,128]{1,0:T(8,128)}, u32[]{:S(2)}) copy-start(f32[16392,128]{1,0:T(8,128)} %pad_convert_fusion) | copy-start | bytes 25178116
  71.2 15.0 %copy-start.10 = (bf16[512,256]{1,0:T(8,128)(2,1)S(1)}, bf16[512,256]{1,0:T(8,128)(2,1)}, u32[]{:S(2)}) copy-start(bf16[512,256]{1,0:T(8,128)(2,1)} %copy-done.9) | copy-start | bytes 786436
  71.2 15.0 %copy-start.12 = (bf16[1024,256]{1,0:T(8,128)(2,1)S(1)}, bf16[1024,256]{1,0:T(8,128)(2,1)}, u32[]{:S(2)}) copy-start(bf16[1024,256]{1,0:T(8,128)(2,1)} %copy-done.11) | copy-start | bytes 1572868
  86.0 14.1 %copy-start.3 = (bf16[1024,256]{1,0:T(8,128)(2,1)S(1)}, bf16[1024,256]{1,0:T(8,128)(2,1)}, u32[]{:S(2)}) copy-start(bf16[1024,256]{1,0:T(8,128)(2,1)} %refs_6_.1) | copy-start | bytes 1572868
  86.0 14.1 %copy-start.4 = (f32[1024]{0:T(1024)S(1)}, f32[1024]{0:T(1024)}, u32[]{:S(2)}) copy-start(f32[1024]{0:T(1024)} %param.14) | copy-start | bytes 12292
  86.1 14.1 %copy-start.5 = (s32[1024]{0:T(1024)S(1)}, s32[1024]{0:T(1024)}, u32[]{:S(2)}) copy-start(s32[1024]{0:T(1024)} %param.19) | copy-start | bytes 12292
  86.1 14.0 %copy-start.6 = (s32[2,16]{1,0:T(2,128)S(1)}, s32[2,16]{1,0:T(2,128)}, u32[]{:S(2)}) copy-start(s32[2,16]{1,0:T(2,128)} %elig_ref.1) | copy-start | bytes 388
  86.1 14.0 %copy-start.7 = (f32[256]{0:T(256)S(1)}, f32[256]{0:T(256)}, u32[]{:S(2)}) copy-start(f32[256]{0:T(256)} %param.16) | copy-start | bytes 3076

commit v4 on v3

--- a/solution.py
+++ b/solution.py
@@ -15,16 +15,17 @@
 
 def pool_kernel(features, bag, ids_ref, table_ref, out_ref, sums_ref):
     users = out_ref.shape[0]
-    width = table_ref.shape[2]
+    width = table_ref.shape[1]
+    row_ref = table_ref.reshape(table_ref.shape[0], 1, width)
 
     def group(step, carry):
         first = pl.multiple_of(step * UNROLL, UNROLL)
         for user in range(UNROLL):
             for feature in range(features):
-                rows = [
-                    table_ref[ids_ref[first + ((feature * bag + entry) * users + user)]]
-                    for entry in range(bag)
-                ]
+                rows = []
+                for entry in range(bag // 2):
+                    pair = ids_ref[first + ((feature * (bag // 2) + entry) * users + user)]
+                    rows += [row_ref[pair & 0xFFFF], row_ref[pair >> 16]]
                 while len(rows) > 1:
                     rows = [
                         rows[k] + rows[k + 1] if k + 1 < len(rows) else rows[k]
@@ -38,7 +39,7 @@
 
 
 def pool_chunk(ids, table, users, features, bag):
-    width = table.shape[2]
+    width = table.shape[1]
     return pl.pallas_call(
         functools.partial(pool_kernel, features, bag),
         out_shape=jax.ShapeDtypeStruct((users, features * width), jnp.bfloat16),
@@ -56,11 +57,12 @@
     )(ids, table)
 
 
-def main_kernel(order, owned, me_ref, elig_ref, *refs):
+def main_kernel(order, owned, chips, me_ref, elig_ref, *refs):
     count = len(order)
-    piece_refs = refs[:count]
-    (w1_ref, b1_ref, w2_ref, b2_ref, mixed_ref, pos_ref, loss_ref, ugrad_ref, igrad_ref,
-     items_ref, scores_ref, signal_ref, acc_ref) = refs[count:]
+    piece_refs, refs = refs[:count], refs[count:]
+    held_refs, refs = refs[:chips], refs[chips:]
+    (w1_ref, b1_ref, w2_ref, b2_ref, pos_ref, loss_ref, ugrad_ref, igrad_ref,
+     items_ref, scores_ref, signal_ref, acc_ref) = refs
     tile = pl.program_id(0)
     tile_users = ugrad_ref.shape[0]
     items = items_ref.shape[0]
@@ -72,9 +74,10 @@
 
     @pl.when(tile == 0)
     def _():
-        for owner in range(items // owned):
-            place = pl.multiple_of((me_ref[1] ^ owner) * owned, owned)
-            items_ref[owner * owned : (owner + 1) * owned, :] = mixed_ref[pl.ds(place, owned), :]
+        for offset in range(items // owned):
+            place = pl.multiple_of((me_ref[1] ^ offset) * owned, owned)
+            lower = offset % 2 * owned
+            items_ref[pl.ds(place, owned), :] = held_refs[offset // 2][lower : lower + owned, :]
 
     hidden = None
     for position, distance in enumerate(order):
@@ -142,16 +145,17 @@
             igrad_ref[h] = acc_ref[:, h * half : (h + 1) * half].astype(igrad_ref.dtype)
 
 
-def main_call(order, owned, me, pieces, w_hidden, b_hidden, w_out, b_out, items, elig, positives):
+def main_call(order, owned, me, pieces, w_hidden, b_hidden, w_out, b_out, held, elig, positives):
     users, depth = pieces[0].shape
     tile_users = 256
     tiles = users // tile_users
-    count, width = items.shape
+    width = w_out.shape[1]
+    count = sum(block.shape[0] for block in held)
     hid = w_hidden.shape[1]
     whole = lambda shape: pl.BlockSpec(shape, lambda i: (0, 0))
     smem = pl.BlockSpec(memory_space=pltpu.SMEM)
     return pl.pallas_call(
-        functools.partial(main_kernel, order, owned),
+        functools.partial(main_kernel, order, owned, len(held)),
         grid=(tiles,),
         out_shape=(
             jax.ShapeDtypeStruct((1, users), jnp.float32),
@@ -160,12 +164,12 @@
         ),
         in_specs=[smem, smem]
         + [pl.BlockSpec((tile_users, depth), lambda i: (i, 0))] * len(order)
+        + [whole(block.shape) for block in held]
         + [
             whole(w_hidden.shape),
             whole((1, hid)),
             whole(w_out.shape),
             whole((1, width)),
-            whole((count, width)),
             pl.BlockSpec((1, tile_users), lambda i: (0, i)),
         ],
         out_specs=(
@@ -182,8 +186,8 @@
         compiler_params=pltpu.CompilerParams(vmem_limit_bytes=48 * MIB),
         name="tower_and_softmax",
     )(
-        me, elig, *pieces, w_hidden, b_hidden.reshape(1, hid), w_out, b_out.reshape(1, width),
-        items, positives.reshape(1, users),
+        me, elig, *pieces, *held, w_hidden, b_hidden.reshape(1, hid), w_out, b_out.reshape(1, width),
+        positives.reshape(1, users),
     )
 
 
@@ -294,42 +298,37 @@
 
     zero_row = features * rows
     table = jnp.pad(tables.reshape(zero_row, width).astype(jnp.float32), ((0, 8), (0, 0)))
-    table = lax.optimization_barrier(table).reshape(zero_row + 8, 1, width)
     ids = jnp.transpose(feat_ids, (1, 2, 0))
     lens = jnp.transpose(bag_lens, (1, 0))
     in_bag = jnp.arange(bag, dtype=jnp.int32)[None, :, None] < lens[:, None, :]
     base = (jnp.arange(features, dtype=jnp.int32) * rows)[:, None, None]
     ids = jnp.where(in_bag, ids + base, zero_row)
-    ids = jnp.transpose(ids.reshape(features * bag, shards, users), (1, 0, 2))
-    ids = ids.reshape(shards, features * bag * users)
+    assert zero_row < 1 << 15 and bag % 2 == 0
+    ids = ids[:, : bag // 2, :] + (ids[:, bag // 2 :, :] << 16)
+    words = features * bag // 2
+    ids = jnp.transpose(ids.reshape(words, shards, users), (1, 0, 2)).reshape(shards, words * users)
 
     cycle = lax.axis_size("item")
-    items = item_vecs
-    reach = 1
+    swap = lambda value, reach: lax.ppermute(
+        value, "item", [(source, source ^ reach) for source in range(cycle)]
+    )
+    own = jnp.concatenate([item_vecs, swap(item_vecs, 1)])
+    held = [own] + [swap(own, 2 * k) for k in range(1, cycle // 2)]
     order = sorted(range(1, shards), key=lambda d: (abs(2 * d - shards), d)) + [0]
     pieces = []
     for distance in order:
         target = lax.rem(me + distance, shards)
         chunk = lax.dynamic_index_in_dim(ids, target, 0, keepdims=False)
-        arrived = None
-        if reach < cycle:
-            pairs = [(source, source ^ reach) for source in range(cycle)]
-            arrived = lax.ppermute(items, "item", pairs)
-            reach *= 2
         pooled = pool_chunk(chunk, table, users, features, bag)
-        if arrived is not None:
-            arrived, pooled = lax.optimization_barrier((arrived, pooled))
-            items = jnp.concatenate([items, arrived])
         if distance:
             pairs = [(source, (source + distance) % shards) for source in range(shards)]
             pooled = lax.ppermute(pooled, "tbl", pairs)
         pieces.append(pooled)
-    assert reach == cycle
 
     loss, user_grad, partial = main_call(
         tuple(order), item_vecs.shape[0],
         jnp.stack([me, lax.axis_index("item")]).astype(jnp.int32), pieces, w_hidden, b_hidden, w_out, b_out,
-        items, elig_mask, positives,
+        held, elig_mask, positives,
     )
     partial = partial.reshape(2, cycle // 2, 2, item_vecs.shape[0], item_vecs.shape[1] // 2)
     item_grad = reduce_call(partial)

time: 141 us -> 117 us (0.83)
  waiting for transfers between devices: 13.9 us -> 0.02 us
  Pallas kernels: 99.3 us -> 88.9 us
    ppermute x3, waiting for transfers between devices: 13.8 us -> 0.01 us  [local(): pooled = lax.ppermute(pooled, 'tbl', pairs)]
    pallas_call x1, Pallas kernels: 23.8 us -> 15.4 us  [reduce_call(): pl.pallas_call(functools.partial(reduce_kernel, chips, shards), out_shape...]
    pallas_call x4, Pallas kernels: 59.3 us -> 57.1 us  [pool_chunk(): pl.pallas_call(functools.partial(pool_kernel, features, bag), out_shape=j...]
    ppermute x3, starting transfers between devices: 6.48 us -> 8.03 us  [local(): pooled = lax.ppermute(pooled, 'tbl', pairs)]
    ppermute x3 -> x4, starting transfers between devices: 4.7 us -> 3.56 us  [local(): lax.ppermute(value, 'item', [(source, source ^ reach) for source in range...]
    unnamed x27 -> x24, local copies, waits for them, and re-layouts: 8.23 us -> 8.14 us
  transfers between devices with their start and end apart: 6 -> 7, of which waited for: 2 -> 0; matrix products, arithmetic and copies ran while one was open for 5% -> 0% of each run, Pallas kernels for 42% -> 37%
where the time goes in v4:
time: 117 us
  Pallas kernels  88.9 us (76%)
  starting transfers between devices  11.6 us (10%)
  local copies, waits for them, and re-layouts  8.38 us (7%)
  other arithmetic  6.91 us (6%)
    pallas_call x4, Pallas kernels, pool_chunk(): pl.pallas_call(functools.partial(pool_kernel, features, bag), out_shape=j...  57.1 us
    pallas_call x1, Pallas kernels, main_call(): pl.pallas_call(functools.partial(main_kernel, order, owned, len(held)), g...  16.4 us
    pallas_call x1, Pallas kernels, reduce_call(): pl.pallas_call(functools.partial(reduce_kernel, chips, shards), out_shape...  15.4 us
    unnamed x24, local copies, waits for them, and re-layouts  8.14 us
    ppermute x3, starting transfers between devices, local(): pooled = lax.ppermute(pooled, 'tbl', pairs)  8.03 us
    pad x1, other arithmetic, local(): jnp.pad(tables.reshape(zero_row, width).astype(jnp.float32), ((0, 8), (0,...  5.74 us
    ppermute x4, starting transfers between devices, local(): lax.ppermute(value, 'item', [(source, source ^ reach) for source in range...  3.56 us
  transfers between devices with their start and end apart: 7, of which 0 were waited for; matrix products, arithmetic and copies ran while one was open for 0% of the time, Pallas kernels for 37%

profile of v4, /device:TPU:0, one launch (start us, length us, event | category | flops | bytes accessed | tf_op | source)
XLA Modules:
  0.0 116.7 jit_solution(14538783579718150698)
XLA Ops:
  0.7 1.0 bitcast_select_fusion
  1.8 0.1 reshape.35
  1.9 5.7 %pad_convert_fusion.table_ref = f32[16392,128]{1,0:T(8,128)} fusion(bf16[16384,128]{1,0:T(8,128)(2,1)} %bitcast.26), kind=kLoop, calls=%fused_computation | loop fusion | flops 2098176 | bytes 12587008 | tf_op jit(solution)/shard_map/jit(_pad)/pad | solution.py:300
  7.6 0.1 constant_dynamic-slice_fusion
  7.8 3.4 %copy-done = f32[16392,128]{1,0:T(8,128)S(1)} copy-done((f32[16392,128]{1,0:T(8,128)S(1)}, f32[16392,128]{1,0:T(8,128)}, u32[]{:S(2)}) %copy-start) | copy-done | bytes 8392728
  11.1 14.3 %pool_chunk.4 = bf16[1024,256]{1,0:T(8,128)(2,1)S(1)} custom-call(s32[8192]{0:T(1024)S(1)} %bitcast.22, f32[16392,128]{1,0:T(8,128)S(1)} %copy-done), custom_call_target="tpu_custom_call" | custom-call | flops 209715200 | bytes 16777216 | tf_op jit(solution)/shard_map/pool_chunk/pallas_call | solution.py:43
  25.4 4.1 %collective-permute-start = (bf16[1024,256]{1,0:T(8,128)(2,1)S(1)}, bf16[1024,256]{1,0:T(8,128)(2,1)S(1)}, u32[]{:S(2)}, u32[]{:S(2)}) collective-permute-start(bf16[1024,256]{1,0:T(8,128)(2,1)S(1)} %pool_chunk.4), channel_id=1, source_target_pairs={{0,2},{1,3},{2,0},{3,1},{4,6},{5,7},{6,4},{7,5},{8,10},{9,11},{10,... | collective-permute-start | bytes 1572872 | tf_op jit(solution)/shard_map/ppermute | solution.py:325
  29.5 0.0 collective-permute-start.3
  29.5 14.3 %pool_chunk.5 = bf16[1024,256]{1,0:T(8,128)(2,1)S(1)} custom-call(s32[8192]{0:T(1024)S(1)} %bitcast.21, f32[16392,128]{1,0:T(8,128)S(1)} %copy-done.1), custom_call_target="tpu_custom_call" | custom-call | flops 209715200 | bytes 16777216 | tf_op jit(solution)/shard_map/pool_chunk/pallas_call | solution.py:43
  43.8 1.6 %collective-permute-start.1 = (bf16[1024,256]{1,0:T(8,128)(2,1)S(1)}, bf16[1024,256]{1,0:T(8,128)(2,1)S(1)}, u32[]{:S(2)}, u32[]{:S(2)}) collective-permute-start(bf16[1024,256]{1,0:T(8,128)(2,1)S(1)} %pool_chunk.5), channel_id=1, source_target_pairs={{0,1},{1,2},{2,3},{3,0},{4,5},{5,6},{6,7},{7,4},{8,9},{9,10},{10,1... | collective-permute-start | bytes 1572872 | tf_op jit(solution)/shard_map/ppermute | solution.py:325
  45.5 1.6 %collective-permute-start.4 = (bf16[512,256]{1,0:T(8,128)(2,1)S(1)}, bf16[512,256]{1,0:T(8,128)(2,1)S(1)}, u32[]{:S(2)}, u32[]{:S(2)}) collective-permute-start(bf16[512,256]{1,0:T(8,128)(2,1)S(1)} %constant_dynamic-update-slice_fusion.refs_4_), channel_id=1, source_target_pairs={{0,8},{4,12},{8,0},{12,4},{16,24},{20,28},{24,16},{28,20},{1,9},{5... | collective-permute-start | bytes 786440 | tf_op jit(solution)/shard_map/ppermute | solution.py:312
  47.0 14.3 %pool_chunk.6 = bf16[1024,256]{1,0:T(8,128)(2,1)S(1)} custom-call(s32[8192]{0:T(1024)S(1)} %bitcast.20, f32[16392,128]{1,0:T(8,128)S(1)} %copy-done.1), custom_call_target="tpu_custom_call" | custom-call | flops 209715200 | bytes 16777216 | tf_op jit(solution)/shard_map/pool_chunk/pallas_call | solution.py:43
  61.3 2.3 %collective-permute-start.2 = (bf16[1024,256]{1,0:T(8,128)(2,1)S(1)}, bf16[1024,256]{1,0:T(8,128)(2,1)S(1)}, u32[]{:S(2)}, u32[]{:S(2)}) collective-permute-start(bf16[1024,256]{1,0:T(8,128)(2,1)S(1)} %pool_chunk.6), channel_id=1, source_target_pairs={{0,3},{1,0},{2,1},{3,2},{4,7},{5,4},{6,5},{7,6},{8,11},{9,8},{10,9... | collective-permute-start | bytes 1572872 | tf_op jit(solution)/shard_map/ppermute | solution.py:325
  63.6 1.5 %collective-permute-start.5 = (bf16[512,256]{1,0:T(8,128)(2,1)S(1)}, bf16[512,256]{1,0:T(8,128)(2,1)}, u32[]{:S(2)}, u32[]{:S(2)}) collective-permute-start(bf16[512,256]{1,0:T(8,128)(2,1)S(1)} %constant_dynamic-update-slice_fusion.refs_4_), channel_id=1, source_target_pairs={{0,16},{4,20},{8,24},{12,28},{16,0},{20,4},{24,8},{28,12},{1,17},{... | collective-permute-start | bytes 786440 | tf_op jit(solution)/shard_map/ppermute | solution.py:312
  65.2 0.7 copy-done.4
  65.9 0.5 collective-permute-start.6
  66.3 3.4 %copy-done.2 = f32[16392,128]{1,0:T(8,128)S(1)} copy-done((f32[16392,128]{1,0:T(8,128)S(1)}, f32[16392,128]{1,0:T(8,128)}, u32[]{:S(2)}) %copy-start.2) | copy-done | bytes 8392728
  69.7 0.0 copy-start.8
  69.7 0.0 copy-start.9
  69.8 14.3 %pool_chunk.7.refs_3_ = bf16[1024,256]{1,0:T(8,128)(2,1)S(1)} custom-call(s32[8192]{0:T(1024)S(1)} %bitcast.19, f32[16392,128]{1,0:T(8,128)S(1)} %copy-done.2), custom_call_target="tpu_custom_call" | custom-call | flops 209715200 | bytes 16777216 | tf_op jit(solution)/shard_map/pool_chunk/pallas_call | solution.py:43
  84.0 0.1 pad_add_fusion.me_ref
  84.2 16.4 %tower_and_softmax.1 = (f32[1,1024]{1,0:T(1,128)}, f32[1024,256]{1,0:T(8,128)}, bf16[2,2048,128]{2,1,0:T(8,128)(2,1)S(1)}) custom-call(s32[2]{0:T(128)S(1)} %pad_add_fusion.me_ref, s32[2,16]{1,0:T(2,128)S(1)} %copy-done.8, bf16[1024,256]{1,0:T(8,128)(2,1)S(1)} %collective-permute-done.refs_0_, bf16[1024,256]{1,0:T(8,128)(2,1)S(1)} %collective-permute-done.1.refs_1_, ...), custom_call_target="tpu_custom_call" | custom-call | tf_op jit(solution)/shard_map/tower_and_softmax/pallas_call | solution.py:157
  100.6 15.4 %reduce_item_grad.1 = f32[64,256]{1,0:T(8,128)S(1)} custom-call(bf16[2,4,2,256,128]{4,3,2,1,0:T(8,128)(2,1)S(1)} %bitcast.18), custom_call_target="tpu_custom_call" | custom-call | tf_op jit(solution)/shard_map/reduce_item_grad/pallas_call | solution.py:268
  116.0 0.6 copy.15
  (28 shorter events, 0.1 us)
Async XLA Ops:
  7.7 3.4 %copy-start = (f32[16392,128]{1,0:T(8,128)S(1)}, f32[16392,128]{1,0:T(8,128)}, u32[]{:S(2)}) copy-start(f32[16392,128]{1,0:T(8,128)} %pad_convert_fusion.table_ref) | copy-start | bytes 25178116
  11.1 18.4 %copy-start.10 = (bf16[256,256]{1,0:T(8,128)(2,1)S(1)}, bf16[256,256]{1,0:T(8,128)(2,1)}, u32[]{:S(2)}) copy-start(bf16[256,256]{1,0:T(8,128)(2,1)} %param.17) | copy-start | bytes 393220
  11.1 18.4 %copy-start.1 = (f32[16392,128]{1,0:T(8,128)S(1)}, f32[16392,128]{1,0:T(8,128)}, u32[]{:S(2)}) copy-start(f32[16392,128]{1,0:T(8,128)} %pad_convert_fusion.table_ref) | copy-start | bytes 25178116
  25.4 58.7 %collective-permute-start = (bf16[1024,256]{1,0:T(8,128)(2,1)S(1)}, bf16[1024,256]{1,0:T(8,128)(2,1)S(1)}, u32[]{:S(2)}, u32[]{:S(2)}) collective-permute-start(bf16[1024,256]{1,0:T(8,128)(2,1)S(1)} %pool_chunk.4), channel_id=1, source_target_pairs={{0,2},{1,3},{2,0},{3,1},{4,6},{5,7},{6,4},{7,5},{8,10},{9,11},{10,... | collective-permute-start | bytes 1572872 | tf_op jit(solution)/shard_map/ppermute | solution.py:325
  29.5 15.9 %collective-permute-start.3 = (bf16[256,256]{1,0:T(8,128)(2,1)S(1)}, bf16[256,256]{1,0:T(8,128)(2,1)S(1)}, u32[]{:S(2)}, u32[]{:S(2)}) collective-permute-start(bf16[256,256]{1,0:T(8,128)(2,1)S(1)} %copy-done.10), channel_id=1, source_target_pairs={{0,4},{4,0},{8,12},{12,8},{16,20},{20,16},{24,28},{28,24},{1,5},{5... | collective-permute-start | bytes 393224 | tf_op jit(solution)/shard_map/ppermute | solution.py:312
  43.8 40.3 %collective-permute-start.1 = (bf16[1024,256]{1,0:T(8,128)(2,1)S(1)}, bf16[1024,256]{1,0:T(8,128)(2,1)S(1)}, u32[]{:S(2)}, u32[]{:S(2)}) collective-permute-start(bf16[1024,256]{1,0:T(8,128)(2,1)S(1)} %pool_chunk.5), channel_id=1, source_target_pairs={{0,1},{1,2},{2,3},{3,0},{4,5},{5,6},{6,7},{7,4},{8,9},{9,10},{10,1... | collective-permute-start | bytes 1572872 | tf_op jit(solution)/shard_map/ppermute | solution.py:325
  45.5 19.7 %collective-permute-start.4 = (bf16[512,256]{1,0:T(8,128)(2,1)S(1)}, bf16[512,256]{1,0:T(8,128)(2,1)S(1)}, u32[]{:S(2)}, u32[]{:S(2)}) collective-permute-start(bf16[512,256]{1,0:T(8,128)(2,1)S(1)} %constant_dynamic-update-slice_fusion.refs_4_), channel_id=1, source_target_pairs={{0,8},{4,12},{8,0},{12,4},{16,24},{20,28},{24,16},{28,20},{1,9},{5... | collective-permute-start | bytes 786440 | tf_op jit(solution)/shard_map/ppermute | solution.py:312
  61.3 22.8 %collective-permute-start.2 = (bf16[1024,256]{1,0:T(8,128)(2,1)S(1)}, bf16[1024,256]{1,0:T(8,128)(2,1)S(1)}, u32[]{:S(2)}, u32[]{:S(2)}) collective-permute-start(bf16[1024,256]{1,0:T(8,128)(2,1)S(1)} %pool_chunk.6), channel_id=1, source_target_pairs={{0,3},{1,0},{2,1},{3,2},{4,7},{5,4},{6,5},{7,6},{8,11},{9,8},{10,9... | collective-permute-start | bytes 1572872 | tf_op jit(solution)/shard_map/ppermute | solution.py:325
  63.6 20.5 %collective-permute-start.5 = (bf16[512,256]{1,0:T(8,128)(2,1)S(1)}, bf16[512,256]{1,0:T(8,128)(2,1)}, u32[]{:S(2)}, u32[]{:S(2)}) collective-permute-start(bf16[512,256]{1,0:T(8,128)(2,1)S(1)} %constant_dynamic-update-slice_fusion.refs_4_), channel_id=1, source_target_pairs={{0,16},{4,20},{8,24},{12,28},{16,0},{20,4},{24,8},{28,12},{1,17},{... | collective-permute-start | bytes 786440 | tf_op jit(solution)/shard_map/ppermute | solution.py:312
  65.2 0.7 copy-start.4
  65.9 18.3 %collective-permute-start.6 = (bf16[512,256]{1,0:T(8,128)(2,1)S(1)}, bf16[512,256]{1,0:T(8,128)(2,1)}, u32[]{:S(2)}, u32[]{:S(2)}) collective-permute-start(bf16[512,256]{1,0:T(8,128)(2,1)S(1)} %constant_dynamic-update-slice_fusion.refs_4_), channel_id=1, source_target_pairs={{0,24},{4,28},{8,16},{12,20},{16,8},{20,12},{24,0},{28,4},{1,25},{... | collective-permute-start | bytes 786440 | tf_op jit(solution)/shard_map/ppermute | solution.py:312
  66.3 3.4 %copy-start.2 = (f32[16392,128]{1,0:T(8,128)S(1)}, f32[16392,128]{1,0:T(8,128)}, u32[]{:S(2)}) copy-start(f32[16392,128]{1,0:T(8,128)} %pad_convert_fusion.table_ref) | copy-start | bytes 25178116
  69.7 14.4 %copy-start.3 = (bf16[1024,256]{1,0:T(8,128)(2,1)S(1)}, bf16[1024,256]{1,0:T(8,128)(2,1)}, u32[]{:S(2)}) copy-start(bf16[1024,256]{1,0:T(8,128)(2,1)} %refs_10_.1) | copy-start | bytes 1572868
  69.7 14.4 %copy-start.5 = (bf16[512,256]{1,0:T(8,128)(2,1)S(1)}, bf16[512,256]{1,0:T(8,128)(2,1)}, u32[]{:S(2)}) copy-start(bf16[512,256]{1,0:T(8,128)(2,1)} %copy-done.4) | copy-start | bytes 786436
  69.7 14.5 %copy-start.6 = (f32[1024]{0:T(1024)S(1)}, f32[1024]{0:T(1024)}, u32[]{:S(2)}) copy-start(f32[1024]{0:T(1024)} %param.14) | copy-start | bytes 12292
  69.7 14.5 %copy-start.7 = (s32[1024]{0:T(1024)S(1)}, s32[1024]{0:T(1024)}, u32[]{:S(2)}) copy-start(s32[1024]{0:T(1024)} %param.19) | copy-start | bytes 12292
  69.7 14.5 %copy-start.8 = (s32[2,16]{1,0:T(2,128)S(1)}, s32[2,16]{1,0:T(2,128)}, u32[]{:S(2)}) copy-start(s32[2,16]{1,0:T(2,128)} %elig_ref.1) | copy-start | bytes 388
  69.7 14.5 %copy-start.9 = (f32[256]{0:T(256)S(1)}, f32[256]{0:T(256)}, u32[]{:S(2)}) copy-start(f32[256]{0:T(256)} %param.16) | copy-start | bytes 3076

commit v5 on v4

--- a/solution.py
+++ b/solution.py
@@ -147,7 +147,7 @@
 
 def main_call(order, owned, me, pieces, w_hidden, b_hidden, w_out, b_out, held, elig, positives):
     users, depth = pieces[0].shape
-    tile_users = 256
+    tile_users = users // elig.shape[0]
     tiles = users // tile_users
     width = w_out.shape[1]
     count = sum(block.shape[0] for block in held)

time: 117 us -> 115 us (0.983)
  Pallas kernels: 88.9 us -> 86.9 us
    pallas_call x1, Pallas kernels: 16.4 us -> 14.4 us  [main_call(): pl.pallas_call(functools.partial(main_kernel, order, owned, len(held)), g...]
where the time goes in v5:
time: 115 us
  Pallas kernels  86.9 us (76%)
  starting transfers between devices  11.6 us (10%)
  local copies, waits for them, and re-layouts  8.38 us (7%)
  other arithmetic  6.91 us (6%)
    pallas_call x4, Pallas kernels, pool_chunk(): pl.pallas_call(functools.partial(pool_kernel, features, bag), out_shape=j...  57.1 us
    pallas_call x1, Pallas kernels, reduce_call(): pl.pallas_call(functools.partial(reduce_kernel, chips, shards), out_shape...  15.4 us
    pallas_call x1, Pallas kernels, main_call(): pl.pallas_call(functools.partial(main_kernel, order, owned, len(held)), g...  14.4 us
    unnamed x24, local copies, waits for them, and re-layouts  8.14 us
    ppermute x3, starting transfers between devices, local(): pooled = lax.ppermute(pooled, 'tbl', pairs)  8.03 us
    pad x1, other arithmetic, local(): jnp.pad(tables.reshape(zero_row, width).astype(jnp.float32), ((0, 8), (0,...  5.74 us
    ppermute x4, starting transfers between devices, local(): lax.ppermute(value, 'item', [(source, source ^ reach) for source in range...  3.56 us
  transfers between devices with their start and end apart: 7, of which 0 were waited for; matrix products, arithmetic and copies ran while one was open for 0% of the time, Pallas kernels for 37%

profile of v5, /device:TPU:0, one launch (start us, length us, event | category | flops | bytes accessed | tf_op | source)
XLA Modules:
  0.0 114.6 jit_solution(10061632276514625677)
XLA Ops:
  0.7 1.0 bitcast_select_fusion
  1.8 0.1 reshape.35
  1.9 5.7 %pad_convert_fusion.table_ref = f32[16392,128]{1,0:T(8,128)} fusion(bf16[16384,128]{1,0:T(8,128)(2,1)} %bitcast.26), kind=kLoop, calls=%fused_computation | loop fusion | flops 2098176 | bytes 12587008 | tf_op jit(solution)/shard_map/jit(_pad)/pad | solution.py:300
  7.6 0.1 constant_dynamic-slice_fusion
  7.8 3.4 %copy-done = f32[16392,128]{1,0:T(8,128)S(1)} copy-done((f32[16392,128]{1,0:T(8,128)S(1)}, f32[16392,128]{1,0:T(8,128)}, u32[]{:S(2)}) %copy-start) | copy-done | bytes 8392728
  11.1 14.3 %pool_chunk.4 = bf16[1024,256]{1,0:T(8,128)(2,1)S(1)} custom-call(s32[8192]{0:T(1024)S(1)} %bitcast.22, f32[16392,128]{1,0:T(8,128)S(1)} %copy-done), custom_call_target="tpu_custom_call" | custom-call | flops 209715200 | bytes 16777216 | tf_op jit(solution)/shard_map/pool_chunk/pallas_call | solution.py:43
  25.4 4.1 %collective-permute-start = (bf16[1024,256]{1,0:T(8,128)(2,1)S(1)}, bf16[1024,256]{1,0:T(8,128)(2,1)S(1)}, u32[]{:S(2)}, u32[]{:S(2)}) collective-permute-start(bf16[1024,256]{1,0:T(8,128)(2,1)S(1)} %pool_chunk.4), channel_id=1, source_target_pairs={{0,2},{1,3},{2,0},{3,1},{4,6},{5,7},{6,4},{7,5},{8,10},{9,11},{10,... | collective-permute-start | bytes 1572872 | tf_op jit(solution)/shard_map/ppermute | solution.py:325
  29.5 14.3 %pool_chunk.5 = bf16[1024,256]{1,0:T(8,128)(2,1)S(1)} custom-call(s32[8192]{0:T(1024)S(1)} %bitcast.21, f32[16392,128]{1,0:T(8,128)S(1)} %copy-done.1), custom_call_target="tpu_custom_call" | custom-call | flops 209715200 | bytes 16777216 | tf_op jit(solution)/shard_map/pool_chunk/pallas_call | solution.py:43
  43.8 1.6 %collective-permute-start.1 = (bf16[1024,256]{1,0:T(8,128)(2,1)S(1)}, bf16[1024,256]{1,0:T(8,128)(2,1)S(1)}, u32[]{:S(2)}, u32[]{:S(2)}) collective-permute-start(bf16[1024,256]{1,0:T(8,128)(2,1)S(1)} %pool_chunk.5), channel_id=1, source_target_pairs={{0,1},{1,2},{2,3},{3,0},{4,5},{5,6},{6,7},{7,4},{8,9},{9,10},{10,1... | collective-permute-start | bytes 1572872 | tf_op jit(solution)/shard_map/ppermute | solution.py:325
  45.5 0.0 collective-permute-done.3
  45.5 1.6 %collective-permute-start.4 = (bf16[512,256]{1,0:T(8,128)(2,1)S(1)}, bf16[512,256]{1,0:T(8,128)(2,1)S(1)}, u32[]{:S(2)}, u32[]{:S(2)}) collective-permute-start(bf16[512,256]{1,0:T(8,128)(2,1)S(1)} %constant_dynamic-update-slice_fusion.refs_4_), channel_id=1, source_target_pairs={{0,8},{4,12},{8,0},{12,4},{16,24},{20,28},{24,16},{28,20},{1,9},{5... | collective-permute-start | bytes 786440 | tf_op jit(solution)/shard_map/ppermute | solution.py:312
  47.0 14.3 %pool_chunk.6 = bf16[1024,256]{1,0:T(8,128)(2,1)S(1)} custom-call(s32[8192]{0:T(1024)S(1)} %bitcast.20, f32[16392,128]{1,0:T(8,128)S(1)} %copy-done.1), custom_call_target="tpu_custom_call" | custom-call | flops 209715200 | bytes 16777216 | tf_op jit(solution)/shard_map/pool_chunk/pallas_call | solution.py:43
  61.3 2.3 %collective-permute-start.2 = (bf16[1024,256]{1,0:T(8,128)(2,1)S(1)}, bf16[1024,256]{1,0:T(8,128)(2,1)S(1)}, u32[]{:S(2)}, u32[]{:S(2)}) collective-permute-start(bf16[1024,256]{1,0:T(8,128)(2,1)S(1)} %pool_chunk.6), channel_id=1, source_target_pairs={{0,3},{1,0},{2,1},{3,2},{4,7},{5,4},{6,5},{7,6},{8,11},{9,8},{10,9... | collective-permute-start | bytes 1572872 | tf_op jit(solution)/shard_map/ppermute | solution.py:325
  63.6 1.5 %collective-permute-start.5 = (bf16[512,256]{1,0:T(8,128)(2,1)S(1)}, bf16[512,256]{1,0:T(8,128)(2,1)}, u32[]{:S(2)}, u32[]{:S(2)}) collective-permute-start(bf16[512,256]{1,0:T(8,128)(2,1)S(1)} %constant_dynamic-update-slice_fusion.refs_4_), channel_id=1, source_target_pairs={{0,16},{4,20},{8,24},{12,28},{16,0},{20,4},{24,8},{28,12},{1,17},{... | collective-permute-start | bytes 786440 | tf_op jit(solution)/shard_map/ppermute | solution.py:312
  65.2 0.7 copy-done.4
  65.9 0.5 collective-permute-start.6
  66.3 3.4 %copy-done.2 = f32[16392,128]{1,0:T(8,128)S(1)} copy-done((f32[16392,128]{1,0:T(8,128)S(1)}, f32[16392,128]{1,0:T(8,128)}, u32[]{:S(2)}) %copy-start.2) | copy-done | bytes 8392728
  69.7 0.0 copy-start.8
  69.7 0.0 copy-start.9
  69.8 14.3 %pool_chunk.7.refs_3_ = bf16[1024,256]{1,0:T(8,128)(2,1)S(1)} custom-call(s32[8192]{0:T(1024)S(1)} %bitcast.19, f32[16392,128]{1,0:T(8,128)S(1)} %copy-done.2), custom_call_target="tpu_custom_call" | custom-call | flops 209715200 | bytes 16777216 | tf_op jit(solution)/shard_map/pool_chunk/pallas_call | solution.py:43
  84.0 0.1 pad_add_fusion.me_ref
  84.2 14.4 %tower_and_softmax.1 = (f32[1,1024]{1,0:T(1,128)}, f32[1024,256]{1,0:T(8,128)}, bf16[2,2048,128]{2,1,0:T(8,128)(2,1)S(1)}) custom-call(s32[2]{0:T(128)S(1)} %pad_add_fusion.me_ref, s32[2,16]{1,0:T(2,128)S(1)} %copy-done.8, bf16[1024,256]{1,0:T(8,128)(2,1)S(1)} %collective-permute-done.refs_0_, bf16[1024,256]{1,0:T(8,128)(2,1)S(1)} %collective-permute-done.1.refs_1_, ...), custom_call_target="tpu_custom_call" | custom-call | tf_op jit(solution)/shard_map/tower_and_softmax/pallas_call | solution.py:157
  98.6 15.4 %reduce_item_grad.1 = f32[64,256]{1,0:T(8,128)S(1)} custom-call(bf16[2,4,2,256,128]{4,3,2,1,0:T(8,128)(2,1)S(1)} %bitcast.18), custom_call_target="tpu_custom_call" | custom-call | tf_op jit(solution)/shard_map/reduce_item_grad/pallas_call | solution.py:268
  114.0 0.6 copy.15
  (28 shorter events, 0.1 us)
Async XLA Ops:
  7.7 3.4 %copy-start = (f32[16392,128]{1,0:T(8,128)S(1)}, f32[16392,128]{1,0:T(8,128)}, u32[]{:S(2)}) copy-start(f32[16392,128]{1,0:T(8,128)} %pad_convert_fusion.table_ref) | copy-start | bytes 25178116
  11.1 18.4 %copy-start.10 = (bf16[256,256]{1,0:T(8,128)(2,1)S(1)}, bf16[256,256]{1,0:T(8,128)(2,1)}, u32[]{:S(2)}) copy-start(bf16[256,256]{1,0:T(8,128)(2,1)} %param.17) | copy-start | bytes 393220
  11.1 18.4 %copy-start.1 = (f32[16392,128]{1,0:T(8,128)S(1)}, f32[16392,128]{1,0:T(8,128)}, u32[]{:S(2)}) copy-start(f32[16392,128]{1,0:T(8,128)} %pad_convert_fusion.table_ref) | copy-start | bytes 25178116
  25.4 58.7 %collective-permute-start = (bf16[1024,256]{1,0:T(8,128)(2,1)S(1)}, bf16[1024,256]{1,0:T(8,128)(2,1)S(1)}, u32[]{:S(2)}, u32[]{:S(2)}) collective-permute-start(bf16[1024,256]{1,0:T(8,128)(2,1)S(1)} %pool_chunk.4), channel_id=1, source_target_pairs={{0,2},{1,3},{2,0},{3,1},{4,6},{5,7},{6,4},{7,5},{8,10},{9,11},{10,... | collective-permute-start | bytes 1572872 | tf_op jit(solution)/shard_map/ppermute | solution.py:325
  29.5 15.9 %collective-permute-start.3 = (bf16[256,256]{1,0:T(8,128)(2,1)S(1)}, bf16[256,256]{1,0:T(8,128)(2,1)S(1)}, u32[]{:S(2)}, u32[]{:S(2)}) collective-permute-start(bf16[256,256]{1,0:T(8,128)(2,1)S(1)} %copy-done.10), channel_id=1, source_target_pairs={{0,4},{4,0},{8,12},{12,8},{16,20},{20,16},{24,28},{28,24},{1,5},{5... | collective-permute-start | bytes 393224 | tf_op jit(solution)/shard_map/ppermute | solution.py:312
  43.8 40.3 %collective-permute-start.1 = (bf16[1024,256]{1,0:T(8,128)(2,1)S(1)}, bf16[1024,256]{1,0:T(8,128)(2,1)S(1)}, u32[]{:S(2)}, u32[]{:S(2)}) collective-permute-start(bf16[1024,256]{1,0:T(8,128)(2,1)S(1)} %pool_chunk.5), channel_id=1, source_target_pairs={{0,1},{1,2},{2,3},{3,0},{4,5},{5,6},{6,7},{7,4},{8,9},{9,10},{10,1... | collective-permute-start | bytes 1572872 | tf_op jit(solution)/shard_map/ppermute | solution.py:325
  45.5 19.7 %collective-permute-start.4 = (bf16[512,256]{1,0:T(8,128)(2,1)S(1)}, bf16[512,256]{1,0:T(8,128)(2,1)S(1)}, u32[]{:S(2)}, u32[]{:S(2)}) collective-permute-start(bf16[512,256]{1,0:T(8,128)(2,1)S(1)} %constant_dynamic-update-slice_fusion.refs_4_), channel_id=1, source_target_pairs={{0,8},{4,12},{8,0},{12,4},{16,24},{20,28},{24,16},{28,20},{1,9},{5... | collective-permute-start | bytes 786440 | tf_op jit(solution)/shard_map/ppermute | solution.py:312
  61.3 22.8 %collective-permute-start.2 = (bf16[1024,256]{1,0:T(8,128)(2,1)S(1)}, bf16[1024,256]{1,0:T(8,128)(2,1)S(1)}, u32[]{:S(2)}, u32[]{:S(2)}) collective-permute-start(bf16[1024,256]{1,0:T(8,128)(2,1)S(1)} %pool_chunk.6), channel_id=1, source_target_pairs={{0,3},{1,0},{2,1},{3,2},{4,7},{5,4},{6,5},{7,6},{8,11},{9,8},{10,9... | collective-permute-start | bytes 1572872 | tf_op jit(solution)/shard_map/ppermute | solution.py:325
  63.6 20.5 %collective-permute-start.5 = (bf16[512,256]{1,0:T(8,128)(2,1)S(1)}, bf16[512,256]{1,0:T(8,128)(2,1)}, u32[]{:S(2)}, u32[]{:S(2)}) collective-permute-start(bf16[512,256]{1,0:T(8,128)(2,1)S(1)} %constant_dynamic-update-slice_fusion.refs_4_), channel_id=1, source_target_pairs={{0,16},{4,20},{8,24},{12,28},{16,0},{20,4},{24,8},{28,12},{1,17},{... | collective-permute-start | bytes 786440 | tf_op jit(solution)/shard_map/ppermute | solution.py:312
  65.2 0.7 copy-start.4
  65.9 18.3 %collective-permute-start.6 = (bf16[512,256]{1,0:T(8,128)(2,1)S(1)}, bf16[512,256]{1,0:T(8,128)(2,1)}, u32[]{:S(2)}, u32[]{:S(2)}) collective-permute-start(bf16[512,256]{1,0:T(8,128)(2,1)S(1)} %constant_dynamic-update-slice_fusion.refs_4_), channel_id=1, source_target_pairs={{0,24},{4,28},{8,16},{12,20},{16,8},{20,12},{24,0},{28,4},{1,25},{... | collective-permute-start | bytes 786440 | tf_op jit(solution)/shard_map/ppermute | solution.py:312
  66.3 3.4 %copy-start.2 = (f32[16392,128]{1,0:T(8,128)S(1)}, f32[16392,128]{1,0:T(8,128)}, u32[]{:S(2)}) copy-start(f32[16392,128]{1,0:T(8,128)} %pad_convert_fusion.table_ref) | copy-start | bytes 25178116
  69.7 14.4 %copy-start.3 = (bf16[1024,256]{1,0:T(8,128)(2,1)S(1)}, bf16[1024,256]{1,0:T(8,128)(2,1)}, u32[]{:S(2)}) copy-start(bf16[1024,256]{1,0:T(8,128)(2,1)} %refs_10_.1) | copy-start | bytes 1572868
  69.7 14.4 %copy-start.5 = (bf16[512,256]{1,0:T(8,128)(2,1)S(1)}, bf16[512,256]{1,0:T(8,128)(2,1)}, u32[]{:S(2)}) copy-start(bf16[512,256]{1,0:T(8,128)(2,1)} %copy-done.4) | copy-start | bytes 786436
  69.7 14.5 %copy-start.6 = (f32[1024]{0:T(1024)S(1)}, f32[1024]{0:T(1024)}, u32[]{:S(2)}) copy-start(f32[1024]{0:T(1024)} %param.14) | copy-start | bytes 12292
  69.7 14.5 %copy-start.7 = (s32[1024]{0:T(1024)S(1)}, s32[1024]{0:T(1024)}, u32[]{:S(2)}) copy-start(s32[1024]{0:T(1024)} %param.19) | copy-start | bytes 12292
  69.7 14.5 %copy-start.8 = (s32[2,16]{1,0:T(2,128)S(1)}, s32[2,16]{1,0:T(2,128)}, u32[]{:S(2)}) copy-start(s32[2,16]{1,0:T(2,128)} %elig_ref.1) | copy-start | bytes 388
  69.7 14.5 %copy-start.9 = (f32[256]{0:T(256)S(1)}, f32[256]{0:T(256)}, u32[]{:S(2)}) copy-start(f32[256]{0:T(256)} %param.16) | copy-start | bytes 3076
